TPU v7x, 512 devices: a whole 4x8x8 slice. The times are simulated.
512 devices in a mesh: rep: 32 (over z, y_lo, core), tp: 16 (over x, y_hi).
Axes of the slice: x: 4, y: 8 (y_hi: 4, y_lo: 2; y = y_hi * 2 + y_lo), z: 8, core: 2. Of those that a mesh axis runs over, the one named last changes fastest.
Arguments:
- projected: bfloat16 [32, 256, 5120], P('rep', None, 'tp'), may hold values from -12 to 12
- serve_order: int32 [32, 256], P('rep'), may hold values from 0 to 255, each once within a row
- key_pool: bfloat16 [32, 512, 64, 512], P('rep', 'tp'), may hold values from -12 to 12
- value_pool: bfloat16 [32, 512, 64, 512], P('rep', 'tp'), may hold values from -4 to 4
- block_table: int32 [32, 256, 8], P('rep', 'tp'), may hold values from 0 to 31
- context_len: int32 [32, 256], P('rep', 'tp'), may hold values from 1 to 512, as said below
- partner: int32 [32], replicated, may hold values from 0 to 31, as said below
- moving_block: int32 [32, 16], P('rep', 'tp'), may hold values from 0 to 31, as said below
Outputs:
- attended: bfloat16 [32, 256, 4096], P('rep', None, 'tp')
Inputs may be any that keep to these rules, and one draw needn't show every extreme that they name: `context_len`: some request of each replica has exactly 512 cached tokens. partner is a perfect matching of the replicas: partner[partner[r]] = r and partner[r] != r. moving_block[r, t] is the first block-table entry of slot t * 16 of replica r.
All inputs are finite; a program needn't handle non-finite values.
Results may differ from a plain program's by a relative error of at most 0.0049.
Values may be sent and summed in bfloat16 or wider, within the bound.
No kernel may reach another device: no remote copies, remote signals or barrier semaphores. Data moves between devices by JAX's collectives and lax.ppermute only.
A program may use at most 128 MiB of HBM per device.

v0:
```python
import jax
import jax.numpy as jnp
from jax import lax
from jax.sharding import PartitionSpec as P

H = 32
KVH = 4
HD = 128


def attend(queries, fresh_keys, fresh_values, keys, values, valid):
    scale = 1.0 / jnp.sqrt(jnp.float32(queries.shape[-1]))
    scores = (
        jnp.einsum("rkgd,rlkd->rkgl", queries, keys, preferred_element_type=jnp.float32) * scale
    )
    fresh = (
        jnp.einsum("rkgd,rkd->rkg", queries, fresh_keys, preferred_element_type=jnp.float32) * scale
    )
    mask = valid[:, None, None, :]
    top = jnp.maximum(jnp.max(jnp.where(mask, scores, -jnp.inf), axis=-1), fresh)
    weights = jnp.where(mask, jnp.exp(scores - top[..., None]), 0.0).astype(jnp.bfloat16)
    own = jnp.exp(fresh - top).astype(jnp.bfloat16).astype(jnp.float32)
    total = jnp.sum(weights.astype(jnp.float32), axis=-1) + own
    numer = jnp.einsum("rkgl,rlkd->rkgd", weights, values, preferred_element_type=jnp.float32)
    numer = numer + own[..., None] * fresh_values.astype(jnp.float32)[:, :, None, :]
    result = (numer / total[..., None]).astype(jnp.bfloat16)
    return result.reshape(result.shape[0], -1)


def body(
    projected, serve_order, key_pool, value_pool, block_table, context_len, partner, moving_block
):
    order_row = serve_order[0]
    group_rows = order_row.shape[0]
    local = projected[0][order_row]
    served = lax.all_to_all(local[None], "tp", split_axis=1, concat_axis=2, tiled=True)[0]
    count = served.shape[0]
    key_blocks = key_pool[0]
    value_blocks = value_pool[0]
    block_len = key_blocks.shape[1]
    tables = block_table[0]
    entries = tables.shape[1]
    lengths = context_len[0]
    block_id = moving_block[0, 0]
    outgoing = jnp.stack([key_blocks[block_id], value_blocks[block_id]])
    mate = partner[lax.axis_index("rep")]
    slots = jnp.zeros((lax.axis_size("rep"),) + outgoing.shape, outgoing.dtype)
    slots = lax.dynamic_update_index_in_dim(slots, outgoing, mate, 0)
    arrived_all = lax.all_to_all(slots, "rep", split_axis=0, concat_axis=0, tiled=True)
    incoming = lax.dynamic_index_in_dim(arrived_all, mate, 0, keepdims=False)
    queries = served[:, : H * HD].reshape(count, KVH, H // KVH, HD)
    fresh_keys = served[:, H * HD : (H + KVH) * HD].reshape(count, KVH, HD)
    fresh_values = served[:, (H + KVH) * HD :].reshape(count, KVH, HD)
    positions = jnp.arange(entries * block_len, dtype=jnp.int32)
    valid = positions[None, :] < lengths[:, None]
    new_keys = lax.dynamic_update_index_in_dim(key_blocks, incoming[0], block_id, 0)
    new_values = lax.dynamic_update_index_in_dim(value_blocks, incoming[1], block_id, 0)
    keys = new_keys[tables].reshape(count, entries * block_len, KVH, HD)
    values = new_values[tables].reshape(count, entries * block_len, KVH, HD)
    heads_out = attend(queries, fresh_keys, fresh_values, keys, values, valid)
    returned = lax.all_to_all(heads_out[None], "tp", split_axis=2, concat_axis=1, tiled=True)
    inverse = (
        jnp.zeros((group_rows,), jnp.int32)
        .at[order_row]
        .set(jnp.arange(group_rows, dtype=jnp.int32))
    )
    return returned[:, inverse]


def solution(mesh):
    in_specs = (
        P("rep", None, "tp"),
        P("rep", None),
        P("rep", "tp", None, None),
        P("rep", "tp", None, None),
        P("rep", "tp", None),
        P("rep", "tp"),
        P(),
        P("rep", "tp"),
    )
    out_specs = P("rep", None, "tp")
    return jax.shard_map(body, mesh=mesh, in_specs=in_specs, out_specs=out_specs, check_vma=False)
```

profile of v0, /device:TPU:128, one launch (start us, length us, event | category | flops | bytes accessed | tf_op | source)
XLA Modules:
  0.0 244.8 jit_solution(1070483020056184160)
XLA Ops:
  0.0 0.0 copy-start.2
  0.0 0.0 copy-start.4
  0.0 0.0 copy-start.1
  0.0 1.7 copy.73
  1.8 0.5 copy-done.1
  2.3 0.0 copy-start.6
  2.3 1.3 copy.74
  3.6 0.0 copy-done.4
  3.6 0.0 copy-done.2
  3.6 0.2 copy.37
  3.8 1.2 gather_fusion
  5.0 0.3 copy.66
  5.3 0.5 broadcast.83
  5.8 1.9 reduce
  7.7 0.9 reshape.163
  8.6 9.7 %all-to-all-start = ((bf16[16,2,2560]{2,1,0:T(2,128)(2,1)}), bf16[16,2,2560]{2,1,0:T(2,128)(2,1)S(1)}, u32[]{:S(2)}, u32[]{:S(2)}) async-start(bf16[16,2,2560]{2,1,0:T(2,128)(2,1)} %reshape.163), calls=%async_computation | async-start | bytes 327680 | tf_op jit(solution)/shard_map/all_to_all | solution.py:36
  18.3 0.0 copy-done.6
  18.3 0.6 dynamic_slice.21
  21.4 0.9 dynamic-slice_bitcast_fusion.2
  22.3 2.5 %broadcast_in_dim.46 = bf16[32,2,64,512]{3,2,1,0:T(8,128)(2,1)} broadcast(bf16[]{:T(256)} %constant.14.clone.1), dimensions={} | broadcast | bytes 4194306 | tf_op jit(solution)/shard_map/broadcast_in_dim | solution.py:47
  24.8 0.7 fusion.16
  25.4 0.0 copy-start.3
  25.4 0.0 copy-start.5
  25.4 4.1 %all-to-all-done = bf16[16,2,2560]{2,1,0:T(2,128)(2,1)S(1)} async-done(((bf16[16,2,2560]{2,1,0:T(2,128)(2,1)}), bf16[16,2,2560]{2,1,0:T(2,128)(2,1)S(1)}, u32[]{:S(2)}, u32[]{:S(2)}) %all-to-all-start) | async-done | bytes 163872 | tf_op jit(solution)/shard_map/all_to_all | solution.py:36
  29.5 9.8 %all-to-all-start.1 = ((bf16[32,2,64,512]{3,2,1,0:T(8,128)(2,1)}), bf16[32,2,64,512]{3,2,1,0:T(8,128)(2,1)}, u32[]{:S(2)}, u32[]{:S(2)}) async-start(bf16[32,2,64,512]{3,2,1,0:T(8,128)(2,1)} %fusion.16), calls=%async_computation.1 | async-start | bytes 8388608 | tf_op jit(solution)/shard_map/all_to_all | solution.py:49
  39.3 0.0 copy-done.3
  39.3 0.1 copy.40
  39.4 0.1 reshape.119
  39.5 1.6 scatter_custom_fusion
  41.1 0.0 copy-done.5
  41.1 0.1 iota_compare_fusion
  41.2 0.3 reshape.164
  41.6 0.2 squeeze.30
  41.9 0.2 fusion.25
  42.1 103.2 %all-to-all-done.1 = bf16[32,2,64,512]{3,2,1,0:T(8,128)(2,1)} async-done(((bf16[32,2,64,512]{3,2,1,0:T(8,128)(2,1)}), bf16[32,2,64,512]{3,2,1,0:T(8,128)(2,1)}, u32[]{:S(2)}, u32[]{:S(2)}) %all-to-all-start.1) | async-done | bytes 4194336 | tf_op jit(solution)/shard_map/all_to_all | solution.py:49
  145.3 1.5 fusion.18
  146.8 6.6 %gather_fusion.1 = bf16[128,64,512]{2,1,0:T(8,128)(2,1)} fusion(bf16[32,64,512]{2,1,0:T(8,128)(2,1)S(1)} %get-tuple-element.7, s32[1024]{0:T(1024)S(1)} %pad_clamp_fusion.1), kind=kCustom, calls=%fused_computation.1 | custom fusion | bytes 16777728 | tf_op jit(solution)/shard_map/gather | solution.py:58
  153.4 12.5 %reshape.105 = bf16[16,512,4,128]{3,2,1,0:T(4,128)(2,1)} reshape(bf16[128,64,512]{2,1,0:T(8,128)(2,1)} %gather_fusion.1) | data formatting | bytes 16777216 | tf_op jit(solution)/shard_map/reshape | solution.py:58
  165.9 0.0 copy-start
  165.9 5.9 %select_reduce_fusion = (f32[16,4,8]{2,1,0:T(4,128)S(1)}, f32[16,4,8,512]{3,2,1,0:T(8,128)S(1)}) fusion(pred[16,512]{1,0:T(8,128)(4,1)S(1)} %iota_compare_fusion, bf16[16,4,8,128]{3,2,1,0:T(8,128)(2,1)S(1)} %bitcast.76, bf16[16,512,4,128]{3,2,1,0:T(4,128)(2,1)} %reshape.105), kind=kOutput, calls=%fused_computation.15 | convolution fusion | flops 67894784 | bytes 9578496 | tf_op jit(solution)/shard_map/rkgd,rlkd->rkgl/dot_general | solution.py:14
  171.8 0.4 convert_reduce_fusion
  172.2 0.0 copy-done
  172.2 6.6 %gather_fusion.2 = bf16[128,64,512]{2,1,0:T(8,128)(2,1)} fusion(bf16[32,64,512]{2,1,0:T(8,128)(2,1)S(1)} %copy-done, s32[1024]{0:T(1024)S(1)} %pad_clamp_fusion.1), kind=kCustom, calls=%fused_computation.2 | custom fusion | bytes 16777728 | tf_op jit(solution)/shard_map/gather | solution.py:59
  178.8 12.5 %reshape.107 = bf16[16,512,4,128]{3,2,1,0:T(4,128)(2,1)} reshape(bf16[128,64,512]{2,1,0:T(8,128)(2,1)} %gather_fusion.2) | data formatting | bytes 16777216 | tf_op jit(solution)/shard_map/reshape | solution.py:59
  191.3 4.7 %fusion.13 = bf16[16,4,8,128]{3,2,1,0:T(8,128)(2,1)S(1)} fusion(bf16[16,512,4,128]{3,2,1,0:T(4,128)(2,1)} %reshape.107, f32[16,4,8]{2,1,0:T(4,128)S(1)} %get-tuple-element.5, f32[16,4,128]{2,1,0:T(4,128)S(1)} %reshape.108, f32[16,4,8]{2,1,0:T(4,128)S(1)} %get-tuple-element.6, f32[16,4,8,512]{3,2,1,0:T(8,128)S(1)} %get-tuple-element.12, ...), kind=kOutput, calls=%fused_computation.12 | convolution fusion | flops 68157440 | bytes 9615360 | tf_op jit(solution)/shard_map/rkgl,rlkd->rkgd/dot_general | solution.py:24
  196.0 0.1 broadcast_in_dim_reshape.3
  196.1 2.7 %copy.43 = bf16[1,16,4096]{1,0,2:T(2,128)(2,1)S(1)} copy(bf16[1,16,4096]{2,1,0:T(8,128)(2,1)S(1)} %broadcast_in_dim_reshape.3) | data formatting | bytes 262144 | tf_op jit(solution)/shard_map/broadcast_in_dim;reshape | solution.py:61
  198.8 22.6 %reduce.1 = bf16[4096,16]{1,0:T(8,128)(2,1)S(1)} reduce(bf16[4096,1,16]{2,1,0:T(2,128)(2,1)S(1)} %bitcast.69, bf16[]{:T(256)} %broadcast.83), dimensions={1}, to_apply=%bitcast.54.reduce_sub_computation | reduce | bytes 262146
  221.5 1.8 reshape.165
  223.2 5.2 %all-to-all-start.2 = ((bf16[16,2,2048]{2,1,0:T(2,128)(2,1)}), bf16[16,2,2048]{2,1,0:T(2,128)(2,1)S(1)}, u32[]{:S(2)}, u32[]{:S(2)}) async-start(bf16[16,2,2048]{2,1,0:T(2,128)(2,1)} %reshape.165), calls=%async_computation.2 | async-start | bytes 262144 | tf_op jit(solution)/shard_map/all_to_all | solution.py:61
  228.5 10.6 %all-to-all-done.2 = bf16[16,2,2048]{2,1,0:T(2,128)(2,1)S(1)} async-done(((bf16[16,2,2048]{2,1,0:T(2,128)(2,1)}), bf16[16,2,2048]{2,1,0:T(2,128)(2,1)S(1)}, u32[]{:S(2)}, u32[]{:S(2)}) %all-to-all-start.2) | async-done | bytes 131104 | tf_op jit(solution)/shard_map/all_to_all | solution.py:61
  239.1 1.8 reshape.166
  240.9 2.0 copy.44
  243.0 1.8 gather_fusion.3
  (19 shorter events, 0.3 us)
Async XLA Ops:
  0.0 3.6 %copy-start.2 = (bf16[1,256,320]{1,2,0:T(8,128)(2,1)S(1)}, bf16[1,256,320]{1,2,0:T(8,128)(2,1)}, u32[]{:S(2)}) copy-start(bf16[1,256,320]{1,2,0:T(8,128)(2,1)} %param.8) | copy-start | bytes 491524
  0.0 3.6 %copy-start.4 = (s32[1,256]{1,0:T(1,128)S(1)}, s32[1,256]{1,0:T(1,128)}, u32[]{:S(2)}) copy-start(s32[1,256]{1,0:T(1,128)} %param.9) | copy-start | bytes 3076
  0.0 2.3 copy-start.1
  2.3 16.0 %copy-start.6 = (s32[32]{0:T(128)S(1)}, s32[32]{0:T(128)}, u32[]{:S(2)}) copy-start(s32[32]{0:T(128)} %param.14) | copy-start | bytes 388
  8.6 20.9 %all-to-all-start = ((bf16[16,2,2560]{2,1,0:T(2,128)(2,1)}), bf16[16,2,2560]{2,1,0:T(2,128)(2,1)S(1)}, u32[]{:S(2)}, u32[]{:S(2)}) async-start(bf16[16,2,2560]{2,1,0:T(2,128)(2,1)} %reshape.163), calls=%async_computation | async-start | bytes 327680 | tf_op jit(solution)/shard_map/all_to_all | solution.py:36
  25.4 13.9 %copy-start.3 = (s32[1,16,8]{1,2,0:T(8,128)S(1)}, s32[1,16,8]{1,2,0:T(8,128)}, u32[]{:S(2)}) copy-start(s32[1,16,8]{1,2,0:T(8,128)} %param.12) | copy-start | bytes 1540
  25.4 15.7 %copy-start.5 = (s32[1,16]{1,0:T(1,128)S(1)}, s32[1,16]{1,0:T(1,128)}, u32[]{:S(2)}) copy-start(s32[1,16]{1,0:T(1,128)} %param.13) | copy-start | bytes 196
  29.5 115.8 %all-to-all-start.1 = ((bf16[32,2,64,512]{3,2,1,0:T(8,128)(2,1)}), bf16[32,2,64,512]{3,2,1,0:T(8,128)(2,1)}, u32[]{:S(2)}, u32[]{:S(2)}) async-start(bf16[32,2,64,512]{3,2,1,0:T(8,128)(2,1)} %fusion.16), calls=%async_computation.1 | async-start | bytes 8388608 | tf_op jit(solution)/shard_map/all_to_all | solution.py:49
  165.9 6.3 %copy-start = (bf16[32,64,512]{2,1,0:T(8,128)(2,1)S(1)}, bf16[32,64,512]{2,1,0:T(8,128)(2,1)}, u32[]{:S(2)}) copy-start(bf16[32,64,512]{2,1,0:T(8,128)(2,1)} %get-tuple-element.8) | copy-start | bytes 6291460
  223.2 15.9 %all-to-all-start.2 = ((bf16[16,2,2048]{2,1,0:T(2,128)(2,1)}), bf16[16,2,2048]{2,1,0:T(2,128)(2,1)S(1)}, u32[]{:S(2)}, u32[]{:S(2)}) async-start(bf16[16,2,2048]{2,1,0:T(2,128)(2,1)} %reshape.165), calls=%async_computation.2 | async-start | bytes 262144 | tf_op jit(solution)/shard_map/all_to_all | solution.py:61
where the time goes:
time: 246 us; the launch traced here: 245 us
  waiting for transfers between devices  118 us (48%)
  local copies, waits for them, and re-layouts  62.9 us (26%)
  other arithmetic  25.7 us (10%)
  starting transfers between devices  24.7 us (10%)
  matrix products  10.8 us (4%)
  between operations  2.84 us (1%)
    all_to_all x1, waiting for transfers between devices, body(): lax.all_to_all(slots, 'rep', split_axis=0, concat_axis=0, tiled=True)  103 us
    unnamed x2, other arithmetic  24.5 us
    reshape x1, local copies, waits for them, and re-layouts, body(): keys = new_keys[tables].reshape(count, entries * block_len, KVH, HD)  12.5 us
    reshape x1, local copies, waits for them, and re-layouts, body(): values = new_values[tables].reshape(count, entries * block_len, KVH, HD)  12.5 us
    all_to_all x1, waiting for transfers between devices, body(): lax.all_to_all(heads_out[None], 'tp', split_axis=2, concat_axis=1, tiled=...  10.6 us
    all_to_all x1, starting transfers between devices, body(): lax.all_to_all(slots, 'rep', split_axis=0, concat_axis=0, tiled=True)  9.83 us
    all_to_all x1, starting transfers between devices, body(): lax.all_to_all(local[None], 'tp', split_axis=1, concat_axis=2, tiled=True)  9.67 us
    unnamed x26, local copies, waits for them, and re-layouts  9.17 us
  transfers between devices with their start and end apart: 3, of which 3 were waited for; matrix products, arithmetic and copies ran while one was open for 3% of the time, Pallas kernels for 0%

commit v1 on v0

v1 whole, which is shorter than its diff:
```python
import math

import jax
import jax.numpy as jnp
from jax import lax
from jax.experimental import pallas as pl
from jax.experimental.pallas import tpu as pltpu
from jax.sharding import PartitionSpec as P

H = 32
KVH = 4
GROUP = H // KVH
HD = 128
BLOCK = 64
NBLK = 32
TBL = 8
ROWS = 16
TOKG = 256
N_TP = 16
FEATS = 320
FRAME = 384
PIECES = 32
TOKENS = NBLK * BLOCK
NEG = -1e30
TO_EXP2 = math.log2(math.e) / math.sqrt(HD)
VMEM = pl.BlockSpec(memory_space=pltpu.VMEM)
SMEM = pl.BlockSpec(memory_space=pltpu.SMEM)
LIMIT = pltpu.CompilerParams(vmem_limit_bytes=40 * 1024 * 1024)


def piece(index):
    rows = (index % 16) // KVH * 16
    cols = index % KVH * HD
    return slice(rows, rows + 16), slice(cols, cols + HD)


def extract_kernel(block_id, keys, values, out):
    for index in range(PIECES):
        source = keys if index < PIECES // 2 else values
        rows, cols = piece(index)
        out[index] = source[0, 0, rows, cols]


def extract(key_pool, value_pool, moving_block):
    spec = pl.BlockSpec((1, 1, BLOCK, KVH * HD), lambda i, block_id: (0, block_id[0, 0], 0, 0))
    return pl.pallas_call(
        extract_kernel,
        out_shape=jax.ShapeDtypeStruct((PIECES, 16, HD), jnp.bfloat16),
        grid_spec=pltpu.PrefetchScalarGridSpec(
            num_scalar_prefetch=1,
            grid=(1,),
            in_specs=[spec, spec],
            out_specs=pl.BlockSpec((PIECES, 16, HD), lambda i, block_id: (0, 0, 0)),
        ),
        name="extract",
    )(moving_block, key_pool, value_pool)


def forward_kernel(partner, got, out):
    for replica in range(PIECES):
        out[replica] = got[partner[replica]]


def forward(partner, got):
    return pl.pallas_call(
        forward_kernel,
        out_shape=jax.ShapeDtypeStruct(got.shape, got.dtype),
        in_specs=[SMEM, VMEM],
        out_specs=VMEM,
        name="forward",
    )(partner, got)


def picks(order):
    request = lax.broadcasted_iota(jnp.int32, (TOKG, TOKG), 0)
    return jnp.where(request == order, 1.0, 0.0).astype(jnp.bfloat16)


def rows_kernel(order, features, out, frame):
    odd = lax.axis_index("tp") % 2
    frame[...] = jnp.zeros_like(frame)
    frame[pl.ds(pl.multiple_of(odd * 64, 64), FEATS), :] = features[0]
    rows = lax.dot_general(
        picks(order[...]), frame[...], (((0,), (1,)), ((), ())), preferred_element_type=jnp.float32
    )
    out[...] = rows.astype(jnp.bfloat16).reshape(out.shape)


def slot_rows(order, projected):
    return pl.pallas_call(
        rows_kernel,
        out_shape=jax.ShapeDtypeStruct((N_TP, ROWS, FRAME), jnp.bfloat16),
        in_specs=[VMEM, VMEM],
        out_specs=VMEM,
        scratch_shapes=[pltpu.VMEM((FRAME, TOKG), jnp.bfloat16)],
        cost_estimate=pl.CostEstimate(flops=2 * TOKG * TOKG * FRAME, bytes_accessed=400000, transcendentals=0),
        name="slot_rows",
    )(order, projected)


def lanes(served, tile):
    pair, place = divmod(tile, 5)
    even, odd = 2 * pair, 2 * pair + 1
    if place < 2:
        return served[even, :, place * HD : (place + 1) * HD]
    if place > 2:
        return served[odd, :, (place - 2) * HD : (place - 1) * HD]
    return served[even, :, 2 * HD : 3 * HD] + served[odd, :, 0:HD]


def counts(tables, lengths, block, offset):
    total = jnp.zeros((ROWS, block.shape[1]), jnp.float32)
    for entry in range(TBL):
        hit = (tables[:, entry : entry + 1] == block) & (offset < lengths - entry * BLOCK)
        total = total + jnp.where(hit, 1.0, 0.0)
    return total


def attend_kernel(block_id, served, keys, values, tables, lengths, numer, stats, queries):
    token = lax.broadcasted_iota(jnp.int32, (1, TOKENS), 1)
    block, offset = token // BLOCK, token % BLOCK
    block = jnp.where(block == block_id[0, 0], -1, block)
    count = counts(tables[0], lengths[...], block, offset)
    kept = count > 0.0
    ones = jnp.ones((TOKENS, HD), jnp.bfloat16)
    for head in range(KVH):
        rows = jnp.concatenate([lanes(served, head * GROUP + g) for g in range(GROUP)], axis=0)
        queries[head] = rows
        fresh_key = lanes(served, H + head).astype(jnp.float32)
        fresh_value = lanes(served, H + KVH + head).astype(jnp.float32)
        cols = slice(head * HD, (head + 1) * HD)
        key = keys[0, :, :, cols].reshape(TOKENS, HD)
        value = values[0, :, :, cols].reshape(TOKENS, HD)
        score = lax.dot_general(rows, key, (((1,), (1,)), ((), ())), preferred_element_type=jnp.float32)
        score = jnp.where(kept[None], score.reshape(GROUP, ROWS, TOKENS), NEG)
        fresh = jnp.sum(
            rows.astype(jnp.float32).reshape(GROUP, ROWS, HD) * fresh_key[None], axis=-1, keepdims=True
        )
        top = jnp.maximum(jnp.max(score, axis=-1, keepdims=True), fresh)
        weight = jnp.exp2((score - top) * TO_EXP2).astype(jnp.bfloat16)
        weight = (weight.astype(jnp.float32) * count[None]).astype(jnp.bfloat16).reshape(GROUP * ROWS, TOKENS)
        both = jnp.dot(weight, jnp.concatenate([value, ones], axis=1), preferred_element_type=jnp.float32)
        own = jnp.exp2((fresh - top) * TO_EXP2).astype(jnp.bfloat16).astype(jnp.float32)
        numer[head] = (both[:, :HD].reshape(GROUP, ROWS, HD) + own * fresh_value[None]).reshape(GROUP * ROWS, HD)
        total = both[:, HD:].reshape(GROUP, ROWS, HD) + own
        half = lax.broadcasted_iota(jnp.int32, (GROUP, ROWS, HD), 2) < HD // 2
        stats[head] = jnp.where(half, top, total).reshape(GROUP * ROWS, HD)


def attend(moving_block, served, key_pool, value_pool, tables, lengths):
    rows = GROUP * ROWS
    return pl.pallas_call(
        attend_kernel,
        out_shape=(
            jax.ShapeDtypeStruct((KVH, rows, HD), jnp.float32),
            jax.ShapeDtypeStruct((KVH, rows, HD), jnp.float32),
            jax.ShapeDtypeStruct((KVH, rows, HD), jnp.bfloat16),
        ),
        in_specs=[SMEM, VMEM, VMEM, VMEM, VMEM, VMEM],
        out_specs=(VMEM, VMEM, VMEM),
        compiler_params=LIMIT,
        cost_estimate=pl.CostEstimate(
            flops=4 * KVH * rows * TOKENS * HD, bytes_accessed=5000000, transcendentals=KVH * rows * TOKENS
        ),
        name="attend",
    )(moving_block, served, key_pool, value_pool, tables, lengths)


def merge_kernel(block_id, arrived, numer, stats, queries, tables, lengths, out):
    offset = lax.broadcasted_iota(jnp.int32, (1, BLOCK), 1)
    count = counts(tables[0], lengths[...], jnp.full((1, BLOCK), block_id[0, 0], jnp.int32), offset)
    kept = count > 0.0
    ones = jnp.ones((BLOCK, HD), jnp.bfloat16)
    for head in range(KVH):
        key = jnp.concatenate([arrived[4 * a + head] for a in range(4)], axis=0)
        value = jnp.concatenate([arrived[16 + 4 * a + head] for a in range(4)], axis=0)
        score = lax.dot_general(
            queries[head], key, (((1,), (1,)), ((), ())), preferred_element_type=jnp.float32
        )
        score = jnp.where(kept[None], score.reshape(GROUP, ROWS, BLOCK), NEG)
        stat = stats[head].reshape(GROUP, ROWS, HD)
        before, total = stat[:, :, 0:1], stat[:, :, HD - 1 : HD]
        top = jnp.maximum(jnp.max(score, axis=-1, keepdims=True), before)
        weight = jnp.exp2((score - top) * TO_EXP2).astype(jnp.bfloat16)
        weight = (weight.astype(jnp.float32) * count[None]).astype(jnp.bfloat16).reshape(GROUP * ROWS, BLOCK)
        both = jnp.dot(weight, jnp.concatenate([value, ones], axis=1), preferred_element_type=jnp.float32)
        both = both.reshape(GROUP, ROWS, 2 * HD)
        kept_part = jnp.exp2((before - top) * TO_EXP2)
        result = (numer[head].reshape(GROUP, ROWS, HD) * kept_part + both[:, :, :HD]) / (
            total * kept_part + both[:, :, HD:]
        )
        result = result.astype(jnp.bfloat16)
        for g in range(GROUP):
            out[4 * head + g // 2, :, (g % 2) * HD : (g % 2 + 1) * HD] = result[g]


def merge(moving_block, arrived, numer, stats, queries, tables, lengths):
    return pl.pallas_call(
        merge_kernel,
        out_shape=jax.ShapeDtypeStruct((N_TP, ROWS, 2 * HD), jnp.bfloat16),
        in_specs=[SMEM, VMEM, VMEM, VMEM, VMEM, VMEM, VMEM],
        out_specs=VMEM,
        compiler_params=LIMIT,
        name="merge",
    )(moving_block, arrived, numer, stats, queries, tables, lengths)


def place_kernel(order, returned, out):
    rows = returned[...].reshape(TOKG, 2 * HD)
    out[0] = jnp.dot(picks(order[...]), rows, preferred_element_type=jnp.float32).astype(jnp.bfloat16)


def place(order, returned):
    return pl.pallas_call(
        place_kernel,
        out_shape=jax.ShapeDtypeStruct((1, TOKG, 2 * HD), jnp.bfloat16),
        in_specs=[VMEM, VMEM],
        out_specs=VMEM,
        name="place",
    )(order, returned)


def exchange(slots, axis):
    return lax.all_to_all(slots, axis, split_axis=0, concat_axis=0, tiled=True)


def body(
    projected, serve_order, key_pool, value_pool, block_table, context_len, partner, moving_block
):
    lengths = context_len.reshape(ROWS, 1)
    spread = exchange(extract(key_pool, value_pool, moving_block), "rep")
    served = exchange(slot_rows(serve_order, jnp.swapaxes(projected, 1, 2)), "tp")
    arrived = exchange(forward(partner, spread), "rep")
    numer, stats, queries = attend(moving_block, served, key_pool, value_pool, block_table, lengths)
    heads = merge(moving_block, arrived, numer, stats, queries, block_table, lengths)
    return place(serve_order, exchange(heads, "tp"))


def solution(mesh):
    in_specs = (
        P("rep", None, "tp"),
        P("rep", None),
        P("rep", "tp", None, None),
        P("rep", "tp", None, None),
        P("rep", "tp", None),
        P("rep", "tp"),
        P(),
        P("rep", "tp"),
    )
    out_specs = P("rep", None, "tp")
    return jax.shard_map(body, mesh=mesh, in_specs=in_specs, out_specs=out_specs, check_vma=False)
```

time: 246 us -> 74.4 us (0.30)
  the two profiles are of different devices: /device:TPU:128 before, /device:TPU:8 now
where the time goes in v1:
time: 74.4 us; the launch traced here: 74 us
  starting transfers between devices  24.6 us (33%)
  waiting for transfers between devices  23 us (31%)
  blocking collectives  14.1 us (19%)
  Pallas kernels  9.76 us (13%)
  local copies, waits for them, and re-layouts  1.76 us (2%)
    all_to_all x3, starting transfers between devices, exchange(): return lax.all_to_all(slots, axis, split_axis=0, concat_axis=0, tiled=True)  24.6 us
    all_to_all x3, waiting for transfers between devices, exchange(): return lax.all_to_all(slots, axis, split_axis=0, concat_axis=0, tiled=True)  23 us
    all_to_all x1, blocking collectives, exchange(): return lax.all_to_all(slots, axis, split_axis=0, concat_axis=0, tiled=True)  14.1 us
    pallas_call x1, Pallas kernels, attend(): pl.pallas_call(attend_kernel, out_shape=(jax.ShapeDtypeStruct((KVH, rows,...  1.91 us
    pallas_call x1, Pallas kernels, slot_rows(): pl.pallas_call(rows_kernel, out_shape=jax.ShapeDtypeStruct((N_TP, ROWS, F...  1.89 us
    pallas_call x1, Pallas kernels, place(): pl.pallas_call(place_kernel, out_shape=jax.ShapeDtypeStruct((1, TOKG, 2 *...  1.77 us
    pallas_call x1, Pallas kernels, extract(): pl.pallas_call(extract_kernel, out_shape=jax.ShapeDtypeStruct((PIECES, 16...  1.7 us
    unnamed x11, local copies, waits for them, and re-layouts  1.68 us
  transfers between devices with their start and end apart: 3, of which 3 were waited for; matrix products, arithmetic and copies ran while one was open for 0% of the time, Pallas kernels for 7%

profile of v1, /device:TPU:8, one launch (start us, length us, event | category | flops | bytes accessed | tf_op | source)
XLA Modules:
  0.0 74.0 jit_solution(13955590998248022462)
XLA Ops:
  0.7 0.0 copy-start.4
  0.7 0.0 copy-start.3
  0.7 0.0 copy-start
  0.7 1.7 %extract.1 = bf16[32,16,128]{2,1,0:T(8,128)(2,1)} custom-call(s32[1,1]{1,0:T(1,128)S(6)} %copy.13.block_id, bf16[1,32,64,512]{3,2,1,0:T(8,128)(2,1)} %keys.3, bf16[1,32,64,512]{3,2,1,0:T(8,128)(2,1)} %values.3), custom_call_target="tpu_custom_call" | custom-call | tf_op jit(solution)/shard_map/extract/pallas_call | solution.py:46
  2.4 11.9 %all-to-all-start = ((bf16[32,16,128]{2,1,0:T(8,128)(2,1)}), bf16[32,16,128]{2,1,0:T(8,128)(2,1)S(1)}, u32[]{:S(2)}, u32[]{:S(2)}) async-start(bf16[32,16,128]{2,1,0:T(8,128)(2,1)} %extract.1), calls=%async_computation | async-start | bytes 262144 | tf_op jit(solution)/shard_map/all_to_all | solution.py:224
  14.3 1.9 %slot_rows.1 = bf16[16,16,384]{2,1,0:T(8,128)(2,1)} custom-call(s32[1,256]{1,0:T(1,128)} %order.3, bf16[1,320,256]{2,1,0:T(8,128)(2,1)} %bitcast.2), custom_call_target="tpu_custom_call" | custom-call | flops 50331648 | bytes 400000 | tf_op jit(solution)/shard_map/slot_rows/pallas_call | solution.py:90
  16.2 7.3 %all-to-all-done.got = bf16[32,16,128]{2,1,0:T(8,128)(2,1)S(1)} async-done(((bf16[32,16,128]{2,1,0:T(8,128)(2,1)}), bf16[32,16,128]{2,1,0:T(8,128)(2,1)S(1)}, u32[]{:S(2)}, u32[]{:S(2)}) %all-to-all-start) | async-done | bytes 131104 | tf_op jit(solution)/shard_map/all_to_all | solution.py:224
  23.5 0.0 copy-start.2
  23.5 8.8 %all-to-all-start.2 = ((bf16[16,16,384]{2,1,0:T(8,128)(2,1)}), bf16[16,16,384]{2,1,0:T(8,128)(2,1)S(1)}, u32[]{:S(2)}, u32[]{:S(2)}) async-start(bf16[16,16,384]{2,1,0:T(8,128)(2,1)} %slot_rows.1), calls=%async_computation.2 | async-start | bytes 393216 | tf_op jit(solution)/shard_map/all_to_all | solution.py:224
  32.3 0.0 copy-done.2
  32.3 1.6 %forward.1 = bf16[32,16,128]{2,1,0:T(8,128)(2,1)} custom-call(s32[32]{0:T(128)} %partner.1, bf16[32,16,128]{2,1,0:T(8,128)(2,1)} %copy-done.2), custom_call_target="tpu_custom_call" | custom-call | tf_op jit(solution)/shard_map/forward/pallas_call | solution.py:65
  33.9 10.2 %all-to-all-done.2.served = bf16[16,16,384]{2,1,0:T(8,128)(2,1)S(1)} async-done(((bf16[16,16,384]{2,1,0:T(8,128)(2,1)}), bf16[16,16,384]{2,1,0:T(8,128)(2,1)S(1)}, u32[]{:S(2)}, u32[]{:S(2)}) %all-to-all-start.2) | async-done | bytes 196640 | tf_op jit(solution)/shard_map/all_to_all | solution.py:224
  44.1 3.9 %all-to-all-start.1 = ((bf16[32,16,128]{2,1,0:T(8,128)(2,1)}), bf16[32,16,128]{2,1,0:T(8,128)(2,1)S(1)}, u32[]{:S(2)}, u32[]{:S(2)}) async-start(bf16[32,16,128]{2,1,0:T(8,128)(2,1)} %forward.1), calls=%async_computation.1 | async-start | bytes 262144 | tf_op jit(solution)/shard_map/all_to_all | solution.py:224
  48.0 0.0 copy-done.4
  48.0 0.1 copy.10.lengths
  48.1 0.0 copy-done.3
  48.1 0.1 copy.9.tables
  48.2 0.0 copy-done
  48.2 0.0 copy-start.1
  48.2 1.6 %copy-done.1 = bf16[1,32,64,512]{3,2,1,0:T(8,128)(2,1)S(1)} copy-done((bf16[1,32,64,512]{3,2,1,0:T(8,128)(2,1)S(1)}, bf16[1,32,64,512]{3,2,1,0:T(8,128)(2,1)}, u32[]{:S(2)}) %copy-start.1) | copy-done | bytes 2097176
  49.8 1.9 %attend.1 = (f32[4,128,128]{2,1,0:T(8,128)S(1)}, f32[4,128,128]{2,1,0:T(8,128)S(1)}, bf16[4,128,128]{2,1,0:T(8,128)(2,1)S(1)}) custom-call(s32[1,1]{1,0:T(1,128)S(6)} %copy.13.block_id, bf16[16,16,384]{2,1,0:T(8,128)(2,1)S(1)} %all-to-all-done.2.served, bf16[1,32,64,512]{3,2,1,0:T(8,128)(2,1)S(1)} %copy-done, bf16[1,32,64,512]{3,2,1,0:T(8,128)(2,1)S(1)} %copy-done.1, ...), custom_call_target="tpu_custom_call" | custom-call | flops 536870912 | bytes 5000000 | tf_op jit(solution)/shard_map/attend/pallas_call | solution.py:152
  51.7 5.5 %all-to-all-done.1.arrived = bf16[32,16,128]{2,1,0:T(8,128)(2,1)S(1)} async-done(((bf16[32,16,128]{2,1,0:T(8,128)(2,1)}), bf16[32,16,128]{2,1,0:T(8,128)(2,1)S(1)}, u32[]{:S(2)}, u32[]{:S(2)}) %all-to-all-start.1) | async-done | bytes 131104 | tf_op jit(solution)/shard_map/all_to_all | solution.py:224
  57.2 0.9 %merge.1 = bf16[16,16,256]{2,1,0:T(8,128)(2,1)S(1)} custom-call(s32[1,1]{1,0:T(1,128)S(6)} %copy.13.block_id, bf16[32,16,128]{2,1,0:T(8,128)(2,1)S(1)} %all-to-all-done.1.arrived, f32[4,128,128]{2,1,0:T(8,128)S(1)} %get-tuple-element.8.numer, f32[4,128,128]{2,1,0:T(8,128)S(1)} %get-tuple-element.9.stats, bf16[4,128,128]{2,1,0:T(8,128)(2,1)S(1)} %get-tuple-element.10.queries, ...), custom_call_target="tpu_custom_call" | custom-call | tf_op jit(solution)/shard_map/merge/pallas_call | solution.py:198
  58.1 14.1 %all_to_all.20.returned = bf16[16,16,256]{2,1,0:T(8,128)(2,1)} all-to-all(bf16[16,16,256]{2,1,0:T(8,128)(2,1)S(1)} %merge.1), channel_id=1, replica_groups=mesh['rep'=32,'tp'=16] {'tp'}, dimensions={0} | all-to-all | bytes 262144 | tf_op jit(solution)/shard_map/all_to_all | solution.py:224
  72.2 1.8 %place.1 = bf16[1,256,256]{2,1,0:T(8,128)(2,1)} custom-call(s32[1,256]{1,0:T(1,128)} %order.3, bf16[16,16,256]{2,1,0:T(8,128)(2,1)} %all_to_all.20.returned), custom_call_target="tpu_custom_call" | custom-call | tf_op jit(solution)/shard_map/place/pallas_call | solution.py:214
Async XLA Ops:
  0.7 47.3 %copy-start.4 = (s32[1,16]{1,0:T(1,128)S(1)}, s32[1,16]{1,0:T(1,128)}, u32[]{:S(2)}) copy-start(s32[1,16]{1,0:T(1,128)} %param.13) | copy-start | bytes 196
  0.7 47.4 %copy-start.3 = (s32[1,16,8]{1,2,0:T(8,128)S(1)}, s32[1,16,8]{1,2,0:T(8,128)}, u32[]{:S(2)}) copy-start(s32[1,16,8]{1,2,0:T(8,128)} %param.12) | copy-start | bytes 1540
  0.7 47.5 %copy-start = (bf16[1,32,64,512]{3,2,1,0:T(8,128)(2,1)S(1)}, bf16[1,32,64,512]{3,2,1,0:T(8,128)(2,1)}, u32[]{:S(2)}) copy-start(bf16[1,32,64,512]{3,2,1,0:T(8,128)(2,1)} %keys.3) | copy-start | bytes 6291460
  2.4 21.1 %all-to-all-start = ((bf16[32,16,128]{2,1,0:T(8,128)(2,1)}), bf16[32,16,128]{2,1,0:T(8,128)(2,1)S(1)}, u32[]{:S(2)}, u32[]{:S(2)}) async-start(bf16[32,16,128]{2,1,0:T(8,128)(2,1)} %extract.1), calls=%async_computation | async-start | bytes 262144 | tf_op jit(solution)/shard_map/all_to_all | solution.py:224
  23.5 8.8 %copy-start.2 = (bf16[32,16,128]{2,1,0:T(8,128)(2,1)}, bf16[32,16,128]{2,1,0:T(8,128)(2,1)S(1)}, u32[]{:S(2)}) copy-start(bf16[32,16,128]{2,1,0:T(8,128)(2,1)S(1)} %all-to-all-done.got) | copy-start | bytes 393220
  23.5 20.6 %all-to-all-start.2 = ((bf16[16,16,384]{2,1,0:T(8,128)(2,1)}), bf16[16,16,384]{2,1,0:T(8,128)(2,1)S(1)}, u32[]{:S(2)}, u32[]{:S(2)}) async-start(bf16[16,16,384]{2,1,0:T(8,128)(2,1)} %slot_rows.1), calls=%async_computation.2 | async-start | bytes 393216 | tf_op jit(solution)/shard_map/all_to_all | solution.py:224
  44.1 13.1 %all-to-all-start.1 = ((bf16[32,16,128]{2,1,0:T(8,128)(2,1)}), bf16[32,16,128]{2,1,0:T(8,128)(2,1)S(1)}, u32[]{:S(2)}, u32[]{:S(2)}) async-start(bf16[32,16,128]{2,1,0:T(8,128)(2,1)} %forward.1), calls=%async_computation.1 | async-start | bytes 262144 | tf_op jit(solution)/shard_map/all_to_all | solution.py:224
  48.2 1.6 %copy-start.1 = (bf16[1,32,64,512]{3,2,1,0:T(8,128)(2,1)S(1)}, bf16[1,32,64,512]{3,2,1,0:T(8,128)(2,1)}, u32[]{:S(2)}) copy-start(bf16[1,32,64,512]{3,2,1,0:T(8,128)(2,1)} %values.3) | copy-start | bytes 6291460

commit v2 on v1

v2 whole, which is shorter than its diff:
```python
import math

import jax
import jax.numpy as jnp
from jax import lax
from jax.experimental import pallas as pl
from jax.experimental.pallas import tpu as pltpu
from jax.sharding import PartitionSpec as P

H = 32
KVH = 4
GROUP = H // KVH
HD = 128
BLOCK = 64
NBLK = 32
TBL = 8
ROWS = 16
TOKG = 256
N_TP = 16
FEATS = 320
FRAME = 384
PIECES = 32
SPANS = BLOCK // 16
TOKENS = NBLK * BLOCK
NEG = -1e30
TO_EXP2 = math.log2(math.e) / math.sqrt(HD)
VMEM = pl.BlockSpec(memory_space=pltpu.VMEM)
HBM = pl.BlockSpec(memory_space=pltpu.HBM)
SMEM = pl.BlockSpec(memory_space=pltpu.SMEM)
SMALL = pltpu.CompilerParams(vmem_limit_bytes=8 * 1024 * 1024)
LARGE = pltpu.CompilerParams(vmem_limit_bytes=24 * 1024 * 1024)


def in_vmem(array):
    return pltpu.with_memory_space_constraint(array, pltpu.VMEM)


def in_hbm(array):
    return pltpu.with_memory_space_constraint(array, pltpu.HBM)


def extract_kernel(block_id, keys, values, out, near, sems):
    copies = []
    for index in range(2 * SPANS):
        pool, span = (keys, values)[index // SPANS], index % SPANS
        copies.append(pltpu.make_async_copy(pool.at[block_id[0, 0], span], near.at[index], sems.at[index]))
        copies[-1].start()
    for index, copy in enumerate(copies):
        copy.wait()
        for head in range(KVH):
            out[KVH * index + head] = near[index, :, head * HD : (head + 1) * HD]


def extract(key_pool, value_pool, moving_block):
    pool = (NBLK, SPANS, 16, KVH * HD)
    return pl.pallas_call(
        extract_kernel,
        out_shape=pltpu.VMEM((PIECES, 16, HD), jnp.bfloat16),
        in_specs=[SMEM, HBM, HBM],
        out_specs=VMEM,
        scratch_shapes=[
            pltpu.VMEM((2 * SPANS, 16, KVH * HD), jnp.bfloat16),
            pltpu.SemaphoreType.DMA((2 * SPANS,)),
        ],
        compiler_params=SMALL,
        name="extract",
    )(moving_block, in_hbm(key_pool.reshape(pool)), in_hbm(value_pool.reshape(pool)))


def forward_kernel(partner, got, out):
    for replica in range(PIECES):
        out[replica] = got[partner[replica]]


def forward(partner, got):
    return pl.pallas_call(
        forward_kernel,
        out_shape=pltpu.VMEM(got.shape, got.dtype),
        in_specs=[SMEM, VMEM],
        out_specs=VMEM,
        compiler_params=SMALL,
        name="forward",
    )(partner, in_vmem(got))


def picks(order):
    request = lax.broadcasted_iota(jnp.int32, (TOKG, TOKG), 0)
    return jnp.where(request == order, 1.0, 0.0).astype(jnp.bfloat16)


def rows_kernel(order, features, out, chosen, frame):
    odd = lax.axis_index("tp") % 2
    frame[...] = jnp.zeros_like(frame)
    frame[pl.ds(pl.multiple_of(odd * 64, 64), FEATS), :] = features[0]
    chosen[...] = picks(order[...])
    rows = lax.dot_general(
        chosen[...], frame[...], (((0,), (1,)), ((), ())), preferred_element_type=jnp.float32
    )
    out[...] = rows.astype(jnp.bfloat16).reshape(out.shape)


def slot_rows(order, projected):
    return pl.pallas_call(
        rows_kernel,
        out_shape=(pltpu.VMEM((N_TP, ROWS, FRAME), jnp.bfloat16), pltpu.VMEM((TOKG, TOKG), jnp.bfloat16)),
        in_specs=[VMEM, VMEM],
        out_specs=(VMEM, VMEM),
        scratch_shapes=[pltpu.VMEM((FRAME, TOKG), jnp.bfloat16)],
        cost_estimate=pl.CostEstimate(flops=2 * TOKG * TOKG * FRAME, bytes_accessed=400000, transcendentals=0),
        compiler_params=SMALL,
        name="slot_rows",
    )(order, projected)


def lanes(served, tile):
    pair, place = divmod(tile, 5)
    even, odd = 2 * pair, 2 * pair + 1
    if place < 2:
        return served[even, :, place * HD : (place + 1) * HD]
    if place > 2:
        return served[odd, :, (place - 2) * HD : (place - 1) * HD]
    return served[even, :, 2 * HD : 3 * HD] + served[odd, :, 0:HD]


def counts(tables, lengths, block, offset):
    total = jnp.zeros((ROWS, block.shape[1]), jnp.float32)
    for entry in range(TBL):
        hit = (tables[:, entry : entry + 1] == block) & (offset < lengths - entry * BLOCK)
        total = total + jnp.where(hit, 1.0, 0.0)
    return total


def attend_kernel(
    block_id, served, keys, value_pool, tables, lengths, numer, tops, totals, queries, moved, values, sem
):
    fetch = pltpu.make_async_copy(value_pool, values, sem)
    fetch.start()
    moved[...] = counts(
        jnp.where(tables[0] == block_id[...], 0, -1), lengths[...], jnp.zeros((1, BLOCK), jnp.int32),
        lax.broadcasted_iota(jnp.int32, (1, BLOCK), 1),
    )
    token = lax.broadcasted_iota(jnp.int32, (1, TOKENS), 1)
    block, offset = token // BLOCK, token % BLOCK
    block = jnp.where(block == block_id[...], -1, block)
    count = counts(tables[0], lengths[...], block, offset)
    kept = count > 0.0
    ones = jnp.ones((TOKENS, HD), jnp.bfloat16)
    for head in range(KVH):
        rows = jnp.concatenate([lanes(served, head * GROUP + g) for g in range(GROUP)], axis=0)
        queries[head] = rows
        fresh_key = lanes(served, H + head).astype(jnp.float32)
        fresh_value = lanes(served, H + KVH + head).astype(jnp.float32)
        cols = slice(head * HD, (head + 1) * HD)
        key = keys[0, :, :, cols].reshape(TOKENS, HD)
        score = lax.dot_general(rows, key, (((1,), (1,)), ((), ())), preferred_element_type=jnp.float32)
        score = jnp.where(kept[None], score.reshape(GROUP, ROWS, TOKENS), NEG)
        fresh = jnp.sum(
            rows.astype(jnp.float32).reshape(GROUP, ROWS, HD) * fresh_key[None], axis=-1, keepdims=True
        )
        top = jnp.maximum(jnp.max(score, axis=-1, keepdims=True), fresh)
        weight = jnp.exp2((score - top) * TO_EXP2).astype(jnp.bfloat16)
        weight = (weight.astype(jnp.float32) * count[None]).astype(jnp.bfloat16).reshape(GROUP * ROWS, TOKENS)
        if head == 0:
            fetch.wait()
        value = values[0, :, :, cols].reshape(TOKENS, HD)
        both = jnp.dot(weight, jnp.concatenate([value, ones], axis=1), preferred_element_type=jnp.float32)
        own = jnp.exp2((fresh - top) * TO_EXP2).astype(jnp.bfloat16).astype(jnp.float32)
        numer[head] = (both[:, :HD].reshape(GROUP, ROWS, HD) + own * fresh_value[None]).reshape(GROUP * ROWS, HD)
        total = both[:, HD:].reshape(GROUP, ROWS, HD) + own
        tops[head] = jnp.broadcast_to(top, (GROUP, ROWS, HD)).reshape(GROUP * ROWS, HD)
        totals[head] = total.reshape(GROUP * ROWS, HD)


def attend(moving_block, served, key_pool, value_pool, tables, lengths):
    rows = GROUP * ROWS
    return pl.pallas_call(
        attend_kernel,
        out_shape=(
            pltpu.VMEM((KVH, rows, HD), jnp.float32),
            pltpu.VMEM((KVH, rows, HD), jnp.float32),
            pltpu.VMEM((KVH, rows, HD), jnp.float32),
            pltpu.VMEM((KVH, rows, HD), jnp.bfloat16),
            pltpu.VMEM((ROWS, BLOCK), jnp.float32),
        ),
        in_specs=[VMEM, VMEM, VMEM, HBM, VMEM, VMEM],
        out_specs=(VMEM,) * 5,
        scratch_shapes=[
            pltpu.VMEM((1, NBLK, BLOCK, KVH * HD), jnp.bfloat16),
            pltpu.SemaphoreType.DMA,
        ],
        compiler_params=LARGE,
        cost_estimate=pl.CostEstimate(
            flops=4 * KVH * rows * TOKENS * HD, bytes_accessed=5000000, transcendentals=KVH * rows * TOKENS
        ),
        name="attend",
    )(moving_block, in_vmem(served), in_vmem(key_pool), in_hbm(value_pool), tables, lengths)


def merge_kernel(arrived, numer, tops, totals, queries, moved, out):
    count = moved[...]
    kept = count > 0.0
    ones = jnp.ones((BLOCK, HD), jnp.bfloat16)
    scores = []
    for head in range(KVH):
        key = jnp.concatenate([arrived[KVH * span + head] for span in range(SPANS)], axis=0)
        score = lax.dot_general(
            queries[head], key, (((1,), (1,)), ((), ())), preferred_element_type=jnp.float32
        )
        scores.append(jnp.where(kept[None], score.reshape(GROUP, ROWS, BLOCK), NEG))
    befores = [tops[head].reshape(GROUP, ROWS, HD) for head in range(KVH)]
    highest = [jnp.max(score, axis=-1, keepdims=True) for score in scores]
    latest = [jnp.maximum(new, old) for new, old in zip(highest, befores)]
    both = []
    for head in range(KVH):
        weight = jnp.exp2((scores[head] - latest[head][:, :, :BLOCK]) * TO_EXP2).astype(jnp.bfloat16)
        weight = (weight.astype(jnp.float32) * count[None]).astype(jnp.bfloat16).reshape(GROUP * ROWS, BLOCK)
        value = jnp.concatenate([arrived[KVH * (SPANS + span) + head] for span in range(SPANS)], axis=0)
        part = jnp.dot(weight, jnp.concatenate([value, ones], axis=1), preferred_element_type=jnp.float32)
        both.append(part.reshape(GROUP, ROWS, 2 * HD))
    results = []
    for head in range(KVH):
        kept_part = jnp.exp2((befores[head] - latest[head]) * TO_EXP2)
        top = numer[head].reshape(GROUP, ROWS, HD) * kept_part + both[head][:, :, :HD]
        bottom = totals[head].reshape(GROUP, ROWS, HD) * kept_part + both[head][:, :, HD:]
        results.append((top / bottom).astype(jnp.bfloat16))
    for head in range(KVH):
        for g in range(GROUP):
            out[4 * head + g // 2, :, (g % 2) * HD : (g % 2 + 1) * HD] = results[head][g]


def merge(arrived, numer, tops, totals, queries, moved):
    return pl.pallas_call(
        merge_kernel,
        out_shape=pltpu.VMEM((N_TP, ROWS, 2 * HD), jnp.bfloat16),
        in_specs=[VMEM] * 6,
        out_specs=VMEM,
        compiler_params=SMALL,
        name="merge",
    )(in_vmem(arrived), numer, tops, totals, queries, moved)


def place_kernel(chosen, returned, out, rows, sems):
    slots = returned[...].reshape(TOKG, 2 * HD)
    half = TOKG // 2
    copies = []
    for part in range(2):
        here = slice(part * half, (part + 1) * half)
        rows[here] = jnp.dot(chosen[here], slots, preferred_element_type=jnp.float32).astype(jnp.bfloat16)
        copies.append(pltpu.make_async_copy(rows.at[here], out.at[0, here], sems.at[part]))
        copies[-1].start()
    for copy in copies:
        copy.wait()


def place(chosen, returned):
    return pl.pallas_call(
        place_kernel,
        out_shape=jax.ShapeDtypeStruct((1, TOKG, 2 * HD), jnp.bfloat16),
        in_specs=[VMEM, VMEM],
        out_specs=HBM,
        scratch_shapes=[pltpu.VMEM((TOKG, 2 * HD), jnp.bfloat16), pltpu.SemaphoreType.DMA((2,))],
        compiler_params=SMALL,
        name="place",
    )(chosen, in_vmem(returned))


def exchange(slots, axis):
    return lax.all_to_all(slots, axis, split_axis=0, concat_axis=0, tiled=True)


def body(
    projected, serve_order, key_pool, value_pool, block_table, context_len, partner, moving_block
):
    lengths = context_len.reshape(ROWS, 1)
    spread = exchange(extract(key_pool, value_pool, moving_block), "rep")
    rows, chosen = slot_rows(serve_order, jnp.swapaxes(projected, 1, 2))
    served = exchange(rows, "tp")
    arrived = exchange(forward(partner, spread), "rep")
    parts = attend(moving_block, served, key_pool, value_pool, block_table, lengths)
    return place(chosen, exchange(merge(arrived, *parts), "tp"))


def solution(mesh):
    in_specs = (
        P("rep", None, "tp"),
        P("rep", None),
        P("rep", "tp", None, None),
        P("rep", "tp", None, None),
        P("rep", "tp", None),
        P("rep", "tp"),
        P(),
        P("rep", "tp"),
    )
    out_specs = P("rep", None, "tp")
    return jax.shard_map(body, mesh=mesh, in_specs=in_specs, out_specs=out_specs, check_vma=False)
```

time: 74.4 us -> 72.7 us (0.977)
  waiting for transfers between devices: 23 us -> 24.6 us
  local copies, waits for them, and re-layouts: 1.76 us -> 0.18 us
  Pallas kernels: 9.76 us -> 8.26 us
    all_to_all x3, waiting for transfers between devices: 23 us -> 24.6 us  [exchange(): return lax.all_to_all(slots, axis, split_axis=0, concat_axis=0, tiled=True)]
    unnamed x11 -> x13, local copies, waits for them, and re-layouts: 1.68 us -> 0.1 us
    pallas_call x1, Pallas kernels: 1.77 us -> 0.86 us  [place(): pl.pallas_call(place_kernel, out_shape=jax.ShapeDtypeStruct((1, TOKG, 2 *...]
where the time goes in v2:
time: 72.7 us; the launch traced here: 72.2 us
  starting transfers between devices  24.6 us (34%)
  waiting for transfers between devices  24.6 us (34%)
  blocking collectives  13.7 us (19%)
  Pallas kernels  8.26 us (11%)
  between operations  0.78 us (1%)
    all_to_all x3, waiting for transfers between devices, exchange(): return lax.all_to_all(slots, axis, split_axis=0, concat_axis=0, tiled=True)  24.6 us
    all_to_all x3, starting transfers between devices, exchange(): return lax.all_to_all(slots, axis, split_axis=0, concat_axis=0, tiled=True)  24.6 us
    all_to_all x1, blocking collectives, exchange(): return lax.all_to_all(slots, axis, split_axis=0, concat_axis=0, tiled=True)  13.7 us
    pallas_call x1, Pallas kernels, attend(): pl.pallas_call(attend_kernel, out_shape=(pltpu.VMEM((KVH, rows, HD), jnp....  3.12 us
    pallas_call x1, Pallas kernels, extract(): pl.pallas_call(extract_kernel, out_shape=pltpu.VMEM((PIECES, 16, HD), jnp...  1.66 us
  transfers between devices with their start and end apart: 3, of which 3 were waited for; matrix products, arithmetic and copies ran while one was open for 0% of the time, Pallas kernels for 7%

profile of v2, /device:TPU:8, one launch (start us, length us, event | category | flops | bytes accessed | tf_op | source)
XLA Modules:
  0.0 72.2 jit_solution(1243080170045354610)
XLA Ops:
  0.7 0.0 copy-start.2
  0.7 0.0 copy-start.3
  0.7 0.0 copy-start.1
  0.7 0.0 copy-start.5
  0.7 0.0 copy-start.4
  0.7 0.0 copy-start
  0.7 1.7 %extract.1 = bf16[32,16,128]{2,1,0:T(8,128)(2,1)} custom-call(s32[1,1]{1,0:T(1,128)S(6)} %copy.11.block_id, bf16[32,4,16,512]{3,2,1,0:T(8,128)(2,1)} %bitcast.4, bf16[32,4,16,512]{3,2,1,0:T(8,128)(2,1)} %bitcast.6), custom_call_target="tpu_custom_call" | custom-call | tf_op jit(solution)/shard_map/extract/pallas_call | solution.py:56
  2.4 11.9 %all-to-all-start = ((bf16[32,16,128]{2,1,0:T(8,128)(2,1)}), bf16[32,16,128]{2,1,0:T(8,128)(2,1)S(1)}, u32[]{:S(2)}, u32[]{:S(2)}) async-start(bf16[32,16,128]{2,1,0:T(8,128)(2,1)} %extract.1), calls=%async_computation | async-start | bytes 262144 | tf_op jit(solution)/shard_map/all_to_all | solution.py:268
  14.3 0.0 copy-done.2
  14.3 0.0 copy-done.3
  14.3 1.0 %slot_rows.1 = (bf16[16,16,384]{2,1,0:T(8,128)(2,1)}, bf16[256,256]{1,0:T(8,128)(2,1)S(1)}) custom-call(s32[1,256]{1,0:T(1,128)S(1)} %copy-done.3, bf16[1,320,256]{2,1,0:T(8,128)(2,1)S(1)} %bitcast.5), custom_call_target="tpu_custom_call" | custom-call | flops 50331648 | bytes 400000 | tf_op jit(solution)/shard_map/slot_rows/pallas_call | solution.py:103
  15.3 8.2 %all-to-all-done.got = bf16[32,16,128]{2,1,0:T(8,128)(2,1)S(1)} async-done(((bf16[32,16,128]{2,1,0:T(8,128)(2,1)}), bf16[32,16,128]{2,1,0:T(8,128)(2,1)S(1)}, u32[]{:S(2)}, u32[]{:S(2)}) %all-to-all-start) | async-done | bytes 131104 | tf_op jit(solution)/shard_map/all_to_all | solution.py:268
  23.5 8.8 %all-to-all-start.2 = ((bf16[16,16,384]{2,1,0:T(8,128)(2,1)}), bf16[16,16,384]{2,1,0:T(8,128)(2,1)S(1)}, u32[]{:S(2)}, u32[]{:S(2)}) async-start(bf16[16,16,384]{2,1,0:T(8,128)(2,1)} %get-tuple-element.13), calls=%async_computation.2 | async-start | bytes 393216 | tf_op jit(solution)/shard_map/all_to_all | solution.py:268
  32.3 0.0 copy-done.1
  32.3 1.2 %forward.1 = bf16[32,16,128]{2,1,0:T(8,128)(2,1)} custom-call(s32[32]{0:T(128)S(1)} %copy-done.1, bf16[32,16,128]{2,1,0:T(8,128)(2,1)S(1)} %all-to-all-done.got), custom_call_target="tpu_custom_call" | custom-call | tf_op jit(solution)/shard_map/forward/pallas_call | solution.py:76
  33.5 10.6 %all-to-all-done.2.served = bf16[16,16,384]{2,1,0:T(8,128)(2,1)S(1)} async-done(((bf16[16,16,384]{2,1,0:T(8,128)(2,1)}), bf16[16,16,384]{2,1,0:T(8,128)(2,1)S(1)}, u32[]{:S(2)}, u32[]{:S(2)}) %all-to-all-start.2) | async-done | bytes 196640 | tf_op jit(solution)/shard_map/all_to_all | solution.py:268
  44.1 3.9 %all-to-all-start.1 = ((bf16[32,16,128]{2,1,0:T(8,128)(2,1)}), bf16[32,16,128]{2,1,0:T(8,128)(2,1)S(1)}, u32[]{:S(2)}, u32[]{:S(2)}) async-start(bf16[32,16,128]{2,1,0:T(8,128)(2,1)} %forward.1), calls=%async_computation.1 | async-start | bytes 262144 | tf_op jit(solution)/shard_map/all_to_all | solution.py:268
  48.0 0.0 copy-done.5
  48.0 0.1 copy.10.lengths
  48.1 0.0 copy-done.4
  48.1 0.1 copy.9.tables
  48.2 0.0 copy-done
  48.2 3.1 %attend.1 = (f32[4,128,128]{2,1,0:T(8,128)S(1)}, f32[4,128,128]{2,1,0:T(8,128)S(1)}, f32[4,128,128]{2,1,0:T(8,128)S(1)}, bf16[4,128,128]{2,1,0:T(8,128)(2,1)S(1)}, f32[16,64]{1,0:T(8,128)S(1)}) custom-call(s32[1,1]{1,0:T(1,128)S(6)} %copy.11.block_id, bf16[16,16,384]{2,1,0:T(8,128)(2,1)S(1)} %all-to-all-done.2.served, bf16[1,32,64,512]{3,2,1,0:T(8,128)(2,1)S(1)} %copy-done, ...), custom_call_target="tpu_custom_call" | custom-call | flops 536870912 | bytes 5000000 | tf_op jit(solution)/shard_map/attend/pallas_call | solution.py:176
  51.3 5.9 %all-to-all-done.1.arrived = bf16[32,16,128]{2,1,0:T(8,128)(2,1)S(1)} async-done(((bf16[32,16,128]{2,1,0:T(8,128)(2,1)}), bf16[32,16,128]{2,1,0:T(8,128)(2,1)S(1)}, u32[]{:S(2)}, u32[]{:S(2)}) %all-to-all-start.1) | async-done | bytes 131104 | tf_op jit(solution)/shard_map/all_to_all | solution.py:268
  57.2 0.4 merge.1
  57.6 13.7 %all_to_all.20.returned = bf16[16,16,256]{2,1,0:T(8,128)(2,1)S(1)} all-to-all(bf16[16,16,256]{2,1,0:T(8,128)(2,1)S(1)} %merge.1), channel_id=1, replica_groups=mesh['rep'=32,'tp'=16] {'tp'}, dimensions={0} | all-to-all | bytes 262144 | tf_op jit(solution)/shard_map/all_to_all | solution.py:268
  71.3 0.9 %place.1 = bf16[1,256,256]{2,1,0:T(8,128)(2,1)} custom-call(bf16[256,256]{1,0:T(8,128)(2,1)S(1)} %get-tuple-element.12.chosen, bf16[16,16,256]{2,1,0:T(8,128)(2,1)S(1)} %all_to_all.20.returned), custom_call_target="tpu_custom_call" | custom-call | tf_op jit(solution)/shard_map/place/pallas_call | solution.py:256
Async XLA Ops:
  0.7 13.7 %copy-start.2 = (bf16[1,256,320]{1,2,0:T(8,128)(2,1)S(1)}, bf16[1,256,320]{1,2,0:T(8,128)(2,1)}, u32[]{:S(2)}) copy-start(bf16[1,256,320]{1,2,0:T(8,128)(2,1)} %param.8) | copy-start | bytes 491524
  0.7 13.7 %copy-start.3 = (s32[1,256]{1,0:T(1,128)S(1)}, s32[1,256]{1,0:T(1,128)}, u32[]{:S(2)}) copy-start(s32[1,256]{1,0:T(1,128)} %order.1) | copy-start | bytes 3076
  0.7 31.6 %copy-start.1 = (s32[32]{0:T(128)S(1)}, s32[32]{0:T(128)}, u32[]{:S(2)}) copy-start(s32[32]{0:T(128)} %partner.1) | copy-start | bytes 388
  0.7 47.3 %copy-start.5 = (s32[1,16]{1,0:T(1,128)S(1)}, s32[1,16]{1,0:T(1,128)}, u32[]{:S(2)}) copy-start(s32[1,16]{1,0:T(1,128)} %param.13) | copy-start | bytes 196
  0.7 47.4 %copy-start.4 = (s32[1,16,8]{1,2,0:T(8,128)S(1)}, s32[1,16,8]{1,2,0:T(8,128)}, u32[]{:S(2)}) copy-start(s32[1,16,8]{1,2,0:T(8,128)} %param.12) | copy-start | bytes 1540
  0.7 47.5 %copy-start = (bf16[1,32,64,512]{3,2,1,0:T(8,128)(2,1)S(1)}, bf16[1,32,64,512]{3,2,1,0:T(8,128)(2,1)}, u32[]{:S(2)}) copy-start(bf16[1,32,64,512]{3,2,1,0:T(8,128)(2,1)} %keys.1) | copy-start | bytes 6291460
  2.4 21.1 %all-to-all-start = ((bf16[32,16,128]{2,1,0:T(8,128)(2,1)}), bf16[32,16,128]{2,1,0:T(8,128)(2,1)S(1)}, u32[]{:S(2)}, u32[]{:S(2)}) async-start(bf16[32,16,128]{2,1,0:T(8,128)(2,1)} %extract.1), calls=%async_computation | async-start | bytes 262144 | tf_op jit(solution)/shard_map/all_to_all | solution.py:268
  23.5 20.6 %all-to-all-start.2 = ((bf16[16,16,384]{2,1,0:T(8,128)(2,1)}), bf16[16,16,384]{2,1,0:T(8,128)(2,1)S(1)}, u32[]{:S(2)}, u32[]{:S(2)}) async-start(bf16[16,16,384]{2,1,0:T(8,128)(2,1)} %get-tuple-element.13), calls=%async_computation.2 | async-start | bytes 393216 | tf_op jit(solution)/shard_map/all_to_all | solution.py:268
  44.1 13.1 %all-to-all-start.1 = ((bf16[32,16,128]{2,1,0:T(8,128)(2,1)}), bf16[32,16,128]{2,1,0:T(8,128)(2,1)S(1)}, u32[]{:S(2)}, u32[]{:S(2)}) async-start(bf16[32,16,128]{2,1,0:T(8,128)(2,1)} %forward.1), calls=%async_computation.1 | async-start | bytes 262144 | tf_op jit(solution)/shard_map/all_to_all | solution.py:268

commit v3 on v2

--- a/solution.py
+++ b/solution.py
@@ -67,20 +67,20 @@
     )(moving_block, in_hbm(key_pool.reshape(pool)), in_hbm(value_pool.reshape(pool)))
 
 
-def forward_kernel(partner, got, out):
+def forward_kernel(partner, got, after, out):
     for replica in range(PIECES):
         out[replica] = got[partner[replica]]
 
 
-def forward(partner, got):
+def forward(partner, got, after):
     return pl.pallas_call(
         forward_kernel,
         out_shape=pltpu.VMEM(got.shape, got.dtype),
-        in_specs=[SMEM, VMEM],
+        in_specs=[SMEM, VMEM, VMEM],
         out_specs=VMEM,
         compiler_params=SMALL,
         name="forward",
-    )(partner, in_vmem(got))
+    )(partner, in_vmem(got), after)
 
 
 def picks(order):
@@ -88,28 +88,57 @@
     return jnp.where(request == order, 1.0, 0.0).astype(jnp.bfloat16)
 
 
-def rows_kernel(order, features, out, chosen, frame):
+def rows_kernel(order, features, out, chosen, frame, near, rows, sems):
     odd = lax.axis_index("tp") % 2
-    frame[...] = jnp.zeros_like(frame)
-    frame[pl.ds(pl.multiple_of(odd * 64, 64), FEATS), :] = features[0]
-    chosen[...] = picks(order[...])
-    rows = lax.dot_general(
-        chosen[...], frame[...], (((0,), (1,)), ((), ())), preferred_element_type=jnp.float32
-    )
-    out[...] = rows.astype(jnp.bfloat16).reshape(out.shape)
+    fetch = [
+        pltpu.make_async_copy(order, near, sems.at[0]),
+        pltpu.make_async_copy(
+            features.at[0], frame.at[pl.ds(pl.multiple_of(odd * 64, 64), FEATS), :], sems.at[1]
+        ),
+    ]
+    for copy in fetch:
+        copy.start()
+    blank = jnp.zeros((FRAME - FEATS, TOKG), jnp.bfloat16)
+    frame[pl.ds(pl.multiple_of((1 - odd) * FEATS, 64), FRAME - FEATS), :] = blank
+    fetch[0].wait()
+    chosen[...] = picks(near[...])
+    fetch[1].wait()
+    send = []
+    for part in range(4):
+        width = TOKG // 4
+        picked = lax.dot_general(
+            chosen[:, part * width : (part + 1) * width],
+            frame[...],
+            (((0,), (1,)), ((), ())),
+            preferred_element_type=jnp.float32,
+        )
+        here = pl.ds(part * N_TP // 4, N_TP // 4)
+        rows[here] = picked.astype(jnp.bfloat16).reshape(N_TP // 4, ROWS, FRAME)
+        send.append(pltpu.make_async_copy(rows.at[here], out.at[here], sems.at[2 + part]))
+        send[-1].start()
+    for copy in send:
+        copy.wait()
 
 
 def slot_rows(order, projected):
     return pl.pallas_call(
         rows_kernel,
-        out_shape=(pltpu.VMEM((N_TP, ROWS, FRAME), jnp.bfloat16), pltpu.VMEM((TOKG, TOKG), jnp.bfloat16)),
-        in_specs=[VMEM, VMEM],
-        out_specs=(VMEM, VMEM),
-        scratch_shapes=[pltpu.VMEM((FRAME, TOKG), jnp.bfloat16)],
+        out_shape=(
+            jax.ShapeDtypeStruct((N_TP, ROWS, FRAME), jnp.bfloat16),
+            pltpu.VMEM((TOKG, TOKG), jnp.bfloat16),
+        ),
+        in_specs=[HBM, HBM],
+        out_specs=(HBM, VMEM),
+        scratch_shapes=[
+            pltpu.VMEM((FRAME, TOKG), jnp.bfloat16),
+            pltpu.VMEM((1, TOKG), jnp.int32),
+            pltpu.VMEM((N_TP, ROWS, FRAME), jnp.bfloat16),
+            pltpu.SemaphoreType.DMA((6,)),
+        ],
         cost_estimate=pl.CostEstimate(flops=2 * TOKG * TOKG * FRAME, bytes_accessed=400000, transcendentals=0),
         compiler_params=SMALL,
         name="slot_rows",
-    )(order, projected)
+    )(in_hbm(order), in_hbm(projected))
 
 
 def lanes(served, tile):
@@ -272,12 +301,12 @@
     projected, serve_order, key_pool, value_pool, block_table, context_len, partner, moving_block
 ):
     lengths = context_len.reshape(ROWS, 1)
-    spread = exchange(extract(key_pool, value_pool, moving_block), "rep")
     rows, chosen = slot_rows(serve_order, jnp.swapaxes(projected, 1, 2))
     served = exchange(rows, "tp")
-    arrived = exchange(forward(partner, spread), "rep")
-    parts = attend(moving_block, served, key_pool, value_pool, block_table, lengths)
-    return place(chosen, exchange(merge(arrived, *parts), "tp"))
+    spread = exchange(extract(key_pool, value_pool, moving_block), "rep")
+    *parts, moved = attend(moving_block, served, key_pool, value_pool, block_table, lengths)
+    arrived = exchange(forward(partner, spread, moved), "rep")
+    return place(chosen, exchange(merge(arrived, *parts, moved), "tp"))
 
 
 def solution(mesh):

time: 72.7 us -> 72.4 us (level)
  blocking collectives: 13.7 us -> 25.9 us
  waiting for transfers between devices: 24.6 us -> 15.6 us
  starting transfers between devices: 24.6 us -> 20.7 us
    all_to_all x1 -> x2, blocking collectives: 13.7 us -> 25.9 us  [exchange(): return lax.all_to_all(slots, axis, split_axis=0, concat_axis=0, tiled=True)]
    all_to_all x3 -> x2, waiting for transfers between devices: 24.6 us -> 15.6 us  [exchange(): return lax.all_to_all(slots, axis, split_axis=0, concat_axis=0, tiled=True)]
    all_to_all x3 -> x2, starting transfers between devices: 24.6 us -> 20.7 us  [exchange(): return lax.all_to_all(slots, axis, split_axis=0, concat_axis=0, tiled=True)]
    pallas_call x1, Pallas kernels: 0.97 us -> 2 us  [slot_rows(): pl.pallas_call(rows_kernel, out_shape=(jax.ShapeDtypeStruct((N_TP, ROWS,...]
  transfers between devices with their start and end apart: 3 -> 2, of which waited for: 3 -> 2; matrix products, arithmetic and copies ran while one was open for 0% -> 0% of each run, Pallas kernels for 7% -> 7%
where the time goes in v3:
time: 72.4 us; the launch traced here: 71.9 us
  blocking collectives  25.9 us (36%)
  starting transfers between devices  20.7 us (29%)
  waiting for transfers between devices  15.6 us (22%)
  Pallas kernels  8.71 us (12%)
  between operations  0.74 us (1%)
    all_to_all x2, blocking collectives, exchange(): return lax.all_to_all(slots, axis, split_axis=0, concat_axis=0, tiled=True)  25.9 us
    all_to_all x2, starting transfers between devices, exchange(): return lax.all_to_all(slots, axis, split_axis=0, concat_axis=0, tiled=True)  20.7 us
    all_to_all x2, waiting for transfers between devices, exchange(): return lax.all_to_all(slots, axis, split_axis=0, concat_axis=0, tiled=True)  15.6 us
    pallas_call x1, Pallas kernels, attend(): pl.pallas_call(attend_kernel, out_shape=(pltpu.VMEM((KVH, rows, HD), jnp....  3.12 us
    pallas_call x1, Pallas kernels, slot_rows(): pl.pallas_call(rows_kernel, out_shape=(jax.ShapeDtypeStruct((N_TP, ROWS,...  2 us
    pallas_call x1, Pallas kernels, extract(): pl.pallas_call(extract_kernel, out_shape=pltpu.VMEM((PIECES, 16, HD), jnp...  1.71 us
  transfers between devices with their start and end apart: 2, of which 2 were waited for; matrix products, arithmetic and copies ran while one was open for 0% of the time, Pallas kernels for 7%

profile of v3, /device:TPU:8, one launch (start us, length us, event | category | flops | bytes accessed | tf_op | source)
XLA Modules:
  0.0 71.9 jit_solution(14771390461129652790)
XLA Ops:
  0.0 2.0 %slot_rows.1 = (bf16[16,16,384]{2,1,0:T(8,128)(2,1)}, bf16[256,256]{1,0:T(8,128)(2,1)S(1)}) custom-call(s32[1,256]{1,0:T(1,128)} %order.1, bf16[1,320,256]{2,1,0:T(8,128)(2,1)} %bitcast.7), custom_call_target="tpu_custom_call" | custom-call | flops 50331648 | bytes 400000 | tf_op jit(solution)/shard_map/slot_rows/pallas_call | solution.py:124
  2.0 8.8 %all-to-all-start.1 = ((bf16[16,16,384]{2,1,0:T(8,128)(2,1)}), bf16[16,16,384]{2,1,0:T(8,128)(2,1)S(1)}, u32[]{:S(2)}, u32[]{:S(2)}) async-start(bf16[16,16,384]{2,1,0:T(8,128)(2,1)} %get-tuple-element.13), calls=%async_computation.1 | async-start | bytes 393216 | tf_op jit(solution)/shard_map/all_to_all | solution.py:297
  11.4 0.0 copy-start.3
  11.5 0.0 copy-start.2
  11.5 0.0 copy-start
  11.5 1.7 %extract.1 = bf16[32,16,128]{2,1,0:T(8,128)(2,1)} custom-call(s32[1,1]{1,0:T(1,128)S(6)} %copy.11.block_id, bf16[32,4,16,512]{3,2,1,0:T(8,128)(2,1)} %bitcast.4, bf16[32,4,16,512]{3,2,1,0:T(8,128)(2,1)} %bitcast.5), custom_call_target="tpu_custom_call" | custom-call | tf_op jit(solution)/shard_map/extract/pallas_call | solution.py:56
  13.2 9.7 %all-to-all-done.1.served = bf16[16,16,384]{2,1,0:T(8,128)(2,1)S(1)} async-done(((bf16[16,16,384]{2,1,0:T(8,128)(2,1)}), bf16[16,16,384]{2,1,0:T(8,128)(2,1)S(1)}, u32[]{:S(2)}, u32[]{:S(2)}) %all-to-all-start.1) | async-done | bytes 196640 | tf_op jit(solution)/shard_map/all_to_all | solution.py:297
  22.9 11.9 %all-to-all-start = ((bf16[32,16,128]{2,1,0:T(8,128)(2,1)}), bf16[32,16,128]{2,1,0:T(8,128)(2,1)S(1)}, u32[]{:S(2)}, u32[]{:S(2)}) async-start(bf16[32,16,128]{2,1,0:T(8,128)(2,1)} %extract.1), calls=%async_computation | async-start | bytes 262144 | tf_op jit(solution)/shard_map/all_to_all | solution.py:297
  34.9 0.0 copy-done.3
  34.9 0.1 copy.10.lengths
  35.0 0.0 copy-done.2
  35.0 0.1 copy.9.tables
  35.1 0.0 copy-done
  35.1 0.0 copy-start.1
  35.1 3.1 %attend.1 = (f32[4,128,128]{2,1,0:T(8,128)S(1)}, f32[4,128,128]{2,1,0:T(8,128)S(1)}, f32[4,128,128]{2,1,0:T(8,128)S(1)}, bf16[4,128,128]{2,1,0:T(8,128)(2,1)S(1)}, f32[16,64]{1,0:T(8,128)S(1)}) custom-call(s32[1,1]{1,0:T(1,128)S(6)} %copy.11.block_id, bf16[16,16,384]{2,1,0:T(8,128)(2,1)S(1)} %all-to-all-done.1.served, bf16[1,32,64,512]{3,2,1,0:T(8,128)(2,1)S(1)} %copy-done, ...), custom_call_target="tpu_custom_call" | custom-call | flops 536870912 | bytes 5000000 | tf_op jit(solution)/shard_map/attend/pallas_call | solution.py:205
  38.2 5.9 %all-to-all-done.got = bf16[32,16,128]{2,1,0:T(8,128)(2,1)S(1)} async-done(((bf16[32,16,128]{2,1,0:T(8,128)(2,1)}), bf16[32,16,128]{2,1,0:T(8,128)(2,1)S(1)}, u32[]{:S(2)}, u32[]{:S(2)}) %all-to-all-start) | async-done | bytes 131104 | tf_op jit(solution)/shard_map/all_to_all | solution.py:297
  44.1 0.0 copy-done.1
  44.1 0.6 forward.1
  44.7 12.5 %all_to_all.20.arrived = bf16[32,16,128]{2,1,0:T(8,128)(2,1)S(1)} all-to-all(bf16[32,16,128]{2,1,0:T(8,128)(2,1)S(1)} %forward.1), channel_id=1, replica_groups=mesh['rep'=32,'tp'=16] {'rep'}, dimensions={0} | all-to-all | bytes 262144 | tf_op jit(solution)/shard_map/all_to_all | solution.py:297
  57.2 0.4 merge.1
  57.7 13.4 %all_to_all.21.returned = bf16[16,16,256]{2,1,0:T(8,128)(2,1)S(1)} all-to-all(bf16[16,16,256]{2,1,0:T(8,128)(2,1)S(1)} %merge.1), channel_id=1, replica_groups=mesh['rep'=32,'tp'=16] {'tp'}, dimensions={0} | all-to-all | bytes 262144 | tf_op jit(solution)/shard_map/all_to_all | solution.py:297
  71.1 0.9 %place.1 = bf16[1,256,256]{2,1,0:T(8,128)(2,1)} custom-call(bf16[256,256]{1,0:T(8,128)(2,1)S(1)} %get-tuple-element.12.chosen, bf16[16,16,256]{2,1,0:T(8,128)(2,1)S(1)} %all_to_all.21.returned), custom_call_target="tpu_custom_call" | custom-call | tf_op jit(solution)/shard_map/place/pallas_call | solution.py:285
Async XLA Ops:
  2.0 20.9 %all-to-all-start.1 = ((bf16[16,16,384]{2,1,0:T(8,128)(2,1)}), bf16[16,16,384]{2,1,0:T(8,128)(2,1)S(1)}, u32[]{:S(2)}, u32[]{:S(2)}) async-start(bf16[16,16,384]{2,1,0:T(8,128)(2,1)} %get-tuple-element.13), calls=%async_computation.1 | async-start | bytes 393216 | tf_op jit(solution)/shard_map/all_to_all | solution.py:297
  11.4 23.4 %copy-start.3 = (s32[1,16]{1,0:T(1,128)S(1)}, s32[1,16]{1,0:T(1,128)}, u32[]{:S(2)}) copy-start(s32[1,16]{1,0:T(1,128)} %param.13) | copy-start | bytes 196
  11.5 23.5 %copy-start.2 = (s32[1,16,8]{1,2,0:T(8,128)S(1)}, s32[1,16,8]{1,2,0:T(8,128)}, u32[]{:S(2)}) copy-start(s32[1,16,8]{1,2,0:T(8,128)} %param.12) | copy-start | bytes 1540
  11.5 23.6 %copy-start = (bf16[1,32,64,512]{3,2,1,0:T(8,128)(2,1)S(1)}, bf16[1,32,64,512]{3,2,1,0:T(8,128)(2,1)}, u32[]{:S(2)}) copy-start(bf16[1,32,64,512]{3,2,1,0:T(8,128)(2,1)} %keys.1) | copy-start | bytes 6291460
  22.9 21.1 %all-to-all-start = ((bf16[32,16,128]{2,1,0:T(8,128)(2,1)}), bf16[32,16,128]{2,1,0:T(8,128)(2,1)S(1)}, u32[]{:S(2)}, u32[]{:S(2)}) async-start(bf16[32,16,128]{2,1,0:T(8,128)(2,1)} %extract.1), calls=%async_computation | async-start | bytes 262144 | tf_op jit(solution)/shard_map/all_to_all | solution.py:297
  35.1 9.0 %copy-start.1 = (s32[32]{0:T(128)S(1)}, s32[32]{0:T(128)}, u32[]{:S(2)}) copy-start(s32[32]{0:T(128)} %partner.1) | copy-start | bytes 388

commit v4 on v3

--- a/solution.py
+++ b/solution.py
@@ -39,7 +39,9 @@
     return pltpu.with_memory_space_constraint(array, pltpu.HBM)
 
 
-def extract_kernel(block_id, keys, values, out, near, sems):
+def extract_kernel(block_id, partner, keys, values, out, mates, near, sems):
+    for replica in range(PIECES):
+        mates[replica] = partner[replica]
     copies = []
     for index in range(2 * SPANS):
         pool, span = (keys, values)[index // SPANS], index % SPANS
@@ -51,20 +53,20 @@
             out[KVH * index + head] = near[index, :, head * HD : (head + 1) * HD]
 
 
-def extract(key_pool, value_pool, moving_block):
+def extract(key_pool, value_pool, moving_block, partner):
     pool = (NBLK, SPANS, 16, KVH * HD)
     return pl.pallas_call(
         extract_kernel,
-        out_shape=pltpu.VMEM((PIECES, 16, HD), jnp.bfloat16),
-        in_specs=[SMEM, HBM, HBM],
-        out_specs=VMEM,
+        out_shape=(pltpu.VMEM((PIECES, 16, HD), jnp.bfloat16), pltpu.SMEM((PIECES,), jnp.int32)),
+        in_specs=[SMEM, SMEM, HBM, HBM],
+        out_specs=(VMEM, SMEM),
         scratch_shapes=[
             pltpu.VMEM((2 * SPANS, 16, KVH * HD), jnp.bfloat16),
             pltpu.SemaphoreType.DMA((2 * SPANS,)),
         ],
         compiler_params=SMALL,
         name="extract",
-    )(moving_block, in_hbm(key_pool.reshape(pool)), in_hbm(value_pool.reshape(pool)))
+    )(moving_block, partner, in_hbm(key_pool.reshape(pool)), in_hbm(value_pool.reshape(pool)))
 
 
 def forward_kernel(partner, got, after, out):
@@ -80,7 +82,7 @@
         out_specs=VMEM,
         compiler_params=SMALL,
         name="forward",
-    )(partner, in_vmem(got), after)
+    )(pltpu.with_memory_space_constraint(partner, pltpu.SMEM), in_vmem(got), after)
 
 
 def picks(order):
@@ -103,21 +105,13 @@
     fetch[0].wait()
     chosen[...] = picks(near[...])
     fetch[1].wait()
-    send = []
-    for part in range(4):
-        width = TOKG // 4
-        picked = lax.dot_general(
-            chosen[:, part * width : (part + 1) * width],
-            frame[...],
-            (((0,), (1,)), ((), ())),
-            preferred_element_type=jnp.float32,
-        )
-        here = pl.ds(part * N_TP // 4, N_TP // 4)
-        rows[here] = picked.astype(jnp.bfloat16).reshape(N_TP // 4, ROWS, FRAME)
-        send.append(pltpu.make_async_copy(rows.at[here], out.at[here], sems.at[2 + part]))
-        send[-1].start()
-    for copy in send:
-        copy.wait()
+    picked = lax.dot_general(
+        chosen[...], frame[...], (((0,), (1,)), ((), ())), preferred_element_type=jnp.float32
+    )
+    rows[...] = picked.astype(jnp.bfloat16).reshape(rows.shape)
+    send = pltpu.make_async_copy(rows, out, sems.at[2])
+    send.start()
+    send.wait()
 
 
 def slot_rows(order, projected):
@@ -133,7 +127,7 @@
             pltpu.VMEM((FRAME, TOKG), jnp.bfloat16),
             pltpu.VMEM((1, TOKG), jnp.int32),
             pltpu.VMEM((N_TP, ROWS, FRAME), jnp.bfloat16),
-            pltpu.SemaphoreType.DMA((6,)),
+            pltpu.SemaphoreType.DMA((3,)),
         ],
         cost_estimate=pl.CostEstimate(flops=2 * TOKG * TOKG * FRAME, bytes_accessed=400000, transcendentals=0),
         compiler_params=SMALL,
@@ -303,9 +297,10 @@
     lengths = context_len.reshape(ROWS, 1)
     rows, chosen = slot_rows(serve_order, jnp.swapaxes(projected, 1, 2))
     served = exchange(rows, "tp")
-    spread = exchange(extract(key_pool, value_pool, moving_block), "rep")
+    pieces, mates = extract(key_pool, value_pool, moving_block, partner)
+    spread = exchange(pieces, "rep")
     *parts, moved = attend(moving_block, served, key_pool, value_pool, block_table, lengths)
-    arrived = exchange(forward(partner, spread, moved), "rep")
+    arrived = exchange(forward(mates, spread, moved), "rep")
     return place(chosen, exchange(merge(arrived, *parts, moved), "tp"))
 
 

time: 72.4 us -> 71.7 us (level)
  waiting for transfers between devices: 15.6 us -> 14.5 us
    all_to_all x2, waiting for transfers between devices: 15.6 us -> 14.5 us  [exchange(): return lax.all_to_all(slots, axis, split_axis=0, concat_axis=0, tiled=True)]
where the time goes in v4:
time: 71.7 us; the launch traced here: 71.3 us
  blocking collectives  26 us (36%)
  starting transfers between devices  20.7 us (29%)
  waiting for transfers between devices  14.5 us (20%)
  Pallas kernels  8.55 us (12%)
  local copies, waits for them, and re-layouts  0.82 us (1%)
  between operations  0.73 us (1%)
    all_to_all x2, blocking collectives, exchange(): return lax.all_to_all(slots, axis, split_axis=0, concat_axis=0, tiled=True)  26 us
    all_to_all x2, starting transfers between devices, exchange(): return lax.all_to_all(slots, axis, split_axis=0, concat_axis=0, tiled=True)  20.7 us
    all_to_all x2, waiting for transfers between devices, exchange(): return lax.all_to_all(slots, axis, split_axis=0, concat_axis=0, tiled=True)  14.5 us
    pallas_call x1, Pallas kernels, attend(): pl.pallas_call(attend_kernel, out_shape=(pltpu.VMEM((KVH, rows, HD), jnp....  3.12 us
    pallas_call x1, Pallas kernels, extract(): pl.pallas_call(extract_kernel, out_shape=(pltpu.VMEM((PIECES, 16, HD), jn...  2.21 us
    pallas_call x1, Pallas kernels, slot_rows(): pl.pallas_call(rows_kernel, out_shape=(jax.ShapeDtypeStruct((N_TP, ROWS,...  1.89 us
  transfers between devices with their start and end apart: 2, of which 2 were waited for; matrix products, arithmetic and copies ran while one was open for 0% of the time, Pallas kernels for 7%

profile of v4, /device:TPU:8, one launch (start us, length us, event | category | flops | bytes accessed | tf_op | source)
XLA Modules:
  0.0 71.3 jit_solution(3646193899634580213)
XLA Ops:
  0.0 1.9 %slot_rows.1 = (bf16[16,16,384]{2,1,0:T(8,128)(2,1)}, bf16[256,256]{1,0:T(8,128)(2,1)S(1)}) custom-call(s32[1,256]{1,0:T(1,128)} %order.1, bf16[1,320,256]{2,1,0:T(8,128)(2,1)} %bitcast.7), custom_call_target="tpu_custom_call" | custom-call | flops 50331648 | bytes 400000 | tf_op jit(solution)/shard_map/slot_rows/pallas_call | solution.py:118
  1.9 8.8 %all-to-all-start.1 = ((bf16[16,16,384]{2,1,0:T(8,128)(2,1)}), bf16[16,16,384]{2,1,0:T(8,128)(2,1)S(1)}, u32[]{:S(2)}, u32[]{:S(2)}) async-start(bf16[16,16,384]{2,1,0:T(8,128)(2,1)} %get-tuple-element.17), calls=%async_computation.1 | async-start | bytes 393216 | tf_op jit(solution)/shard_map/all_to_all | solution.py:291
  11.3 0.0 copy-start.1
  11.3 0.6 copy-done.1
  12.0 0.0 copy-start.3
  12.0 0.0 copy-start.2
  12.0 0.0 copy-start
  12.0 2.2 %extract.1 = (bf16[32,16,128]{2,1,0:T(8,128)(2,1)}, s32[32]{0:T(128)S(4)}) custom-call(s32[1,1]{1,0:T(1,128)S(6)} %copy.11.block_id, s32[32]{0:T(128)S(1)} %copy-done.1, bf16[32,4,16,512]{3,2,1,0:T(8,128)(2,1)} %bitcast.4, bf16[32,4,16,512]{3,2,1,0:T(8,128)(2,1)} %bitcast.5), custom_call_target="tpu_custom_call" | custom-call | tf_op jit(solution)/shard_map/extract/pallas_call | solution.py:58
  14.2 8.6 %all-to-all-done.1.served = bf16[16,16,384]{2,1,0:T(8,128)(2,1)S(1)} async-done(((bf16[16,16,384]{2,1,0:T(8,128)(2,1)}), bf16[16,16,384]{2,1,0:T(8,128)(2,1)S(1)}, u32[]{:S(2)}, u32[]{:S(2)}) %all-to-all-start.1) | async-done | bytes 196640 | tf_op jit(solution)/shard_map/all_to_all | solution.py:291
  22.8 11.9 %all-to-all-start = ((bf16[32,16,128]{2,1,0:T(8,128)(2,1)}), bf16[32,16,128]{2,1,0:T(8,128)(2,1)S(1)}, u32[]{:S(2)}, u32[]{:S(2)}) async-start(bf16[32,16,128]{2,1,0:T(8,128)(2,1)} %get-tuple-element.16), calls=%async_computation | async-start | bytes 262144 | tf_op jit(solution)/shard_map/all_to_all | solution.py:291
  34.8 0.0 copy-done.3
  34.8 0.1 copy.10.lengths
  34.9 0.0 copy-done.2
  34.9 0.1 copy.9.tables
  34.9 0.0 copy-done
  34.9 3.1 %attend.1 = (f32[4,128,128]{2,1,0:T(8,128)S(1)}, f32[4,128,128]{2,1,0:T(8,128)S(1)}, f32[4,128,128]{2,1,0:T(8,128)S(1)}, bf16[4,128,128]{2,1,0:T(8,128)(2,1)S(1)}, f32[16,64]{1,0:T(8,128)S(1)}) custom-call(s32[1,1]{1,0:T(1,128)S(6)} %copy.11.block_id, bf16[16,16,384]{2,1,0:T(8,128)(2,1)S(1)} %all-to-all-done.1.served, bf16[1,32,64,512]{3,2,1,0:T(8,128)(2,1)S(1)} %copy-done, ...), custom_call_target="tpu_custom_call" | custom-call | flops 536870912 | bytes 5000000 | tf_op jit(solution)/shard_map/attend/pallas_call | solution.py:199
  38.1 5.9 %all-to-all-done.got = bf16[32,16,128]{2,1,0:T(8,128)(2,1)S(1)} async-done(((bf16[32,16,128]{2,1,0:T(8,128)(2,1)}), bf16[32,16,128]{2,1,0:T(8,128)(2,1)S(1)}, u32[]{:S(2)}, u32[]{:S(2)}) %all-to-all-start) | async-done | bytes 131104 | tf_op jit(solution)/shard_map/all_to_all | solution.py:291
  44.0 12.5 %all_to_all.20.arrived = bf16[32,16,128]{2,1,0:T(8,128)(2,1)S(1)} all-to-all(bf16[32,16,128]{2,1,0:T(8,128)(2,1)S(1)} %forward.1), channel_id=1, replica_groups=mesh['rep'=32,'tp'=16] {'rep'}, dimensions={0} | all-to-all | bytes 262144 | tf_op jit(solution)/shard_map/all_to_all | solution.py:291
  56.5 0.4 merge.1
  57.0 13.4 %all_to_all.21.returned = bf16[16,16,256]{2,1,0:T(8,128)(2,1)S(1)} all-to-all(bf16[16,16,256]{2,1,0:T(8,128)(2,1)S(1)} %merge.1), channel_id=1, replica_groups=mesh['rep'=32,'tp'=16] {'tp'}, dimensions={0} | all-to-all | bytes 262144 | tf_op jit(solution)/shard_map/all_to_all | solution.py:291
  70.4 0.9 %place.1 = bf16[1,256,256]{2,1,0:T(8,128)(2,1)} custom-call(bf16[256,256]{1,0:T(8,128)(2,1)S(1)} %get-tuple-element.14.chosen, bf16[16,16,256]{2,1,0:T(8,128)(2,1)S(1)} %all_to_all.21.returned), custom_call_target="tpu_custom_call" | custom-call | tf_op jit(solution)/shard_map/place/pallas_call | solution.py:279
  (1 shorter events, 0.0 us)
Async XLA Ops:
  1.9 20.9 %all-to-all-start.1 = ((bf16[16,16,384]{2,1,0:T(8,128)(2,1)}), bf16[16,16,384]{2,1,0:T(8,128)(2,1)S(1)}, u32[]{:S(2)}, u32[]{:S(2)}) async-start(bf16[16,16,384]{2,1,0:T(8,128)(2,1)} %get-tuple-element.17), calls=%async_computation.1 | async-start | bytes 393216 | tf_op jit(solution)/shard_map/all_to_all | solution.py:291
  11.3 0.7 copy-start.1
  12.0 22.8 %copy-start.3 = (s32[1,16]{1,0:T(1,128)S(1)}, s32[1,16]{1,0:T(1,128)}, u32[]{:S(2)}) copy-start(s32[1,16]{1,0:T(1,128)} %param.13) | copy-start | bytes 196
  12.0 22.9 %copy-start.2 = (s32[1,16,8]{1,2,0:T(8,128)S(1)}, s32[1,16,8]{1,2,0:T(8,128)}, u32[]{:S(2)}) copy-start(s32[1,16,8]{1,2,0:T(8,128)} %param.12) | copy-start | bytes 1540
  12.0 23.0 %copy-start = (bf16[1,32,64,512]{3,2,1,0:T(8,128)(2,1)S(1)}, bf16[1,32,64,512]{3,2,1,0:T(8,128)(2,1)}, u32[]{:S(2)}) copy-start(bf16[1,32,64,512]{3,2,1,0:T(8,128)(2,1)} %keys.1) | copy-start | bytes 6291460
  22.8 21.1 %all-to-all-start = ((bf16[32,16,128]{2,1,0:T(8,128)(2,1)}), bf16[32,16,128]{2,1,0:T(8,128)(2,1)S(1)}, u32[]{:S(2)}, u32[]{:S(2)}) async-start(bf16[32,16,128]{2,1,0:T(8,128)(2,1)} %get-tuple-element.16), calls=%async_computation | async-start | bytes 262144 | tf_op jit(solution)/shard_map/all_to_all | solution.py:291

commit v5 on v4

--- a/solution.py
+++ b/solution.py
@@ -85,12 +85,7 @@
     )(pltpu.with_memory_space_constraint(partner, pltpu.SMEM), in_vmem(got), after)
 
 
-def picks(order):
-    request = lax.broadcasted_iota(jnp.int32, (TOKG, TOKG), 0)
-    return jnp.where(request == order, 1.0, 0.0).astype(jnp.bfloat16)
-
-
-def rows_kernel(order, features, out, chosen, frame, near, rows, sems):
+def rows_kernel(order, features, out, chosen, frame, near, rows, by_slot, sems):
     odd = lax.axis_index("tp") % 2
     fetch = [
         pltpu.make_async_copy(order, near, sems.at[0]),
@@ -103,15 +98,26 @@
     blank = jnp.zeros((FRAME - FEATS, TOKG), jnp.bfloat16)
     frame[pl.ds(pl.multiple_of((1 - odd) * FEATS, 64), FRAME - FEATS), :] = blank
     fetch[0].wait()
-    chosen[...] = picks(near[...])
+    request = lax.broadcasted_iota(jnp.int32, (TOKG, TOKG), 0)
+    hits = jnp.where(request == near[...], 1.0, 0.0)
+    chosen[...] = hits.astype(jnp.bfloat16)
+    by_slot[...] = hits.T.astype(jnp.bfloat16)
     fetch[1].wait()
-    picked = lax.dot_general(
-        chosen[...], frame[...], (((0,), (1,)), ((), ())), preferred_element_type=jnp.float32
-    )
-    rows[...] = picked.astype(jnp.bfloat16).reshape(rows.shape)
-    send = pltpu.make_async_copy(rows, out, sems.at[2])
-    send.start()
-    send.wait()
+    send = []
+    for part in range(2):
+        width, slots = TOKG // 2, N_TP // 2
+        picked = lax.dot_general(
+            by_slot[part * width : (part + 1) * width],
+            frame[...],
+            (((1,), (1,)), ((), ())),
+            preferred_element_type=jnp.float32,
+        )
+        here = pl.ds(part * slots, slots)
+        rows[here] = picked.astype(jnp.bfloat16).reshape(slots, ROWS, FRAME)
+        send.append(pltpu.make_async_copy(rows.at[here], out.at[here], sems.at[2 + part]))
+        send[-1].start()
+    for copy in send:
+        copy.wait()
 
 
 def slot_rows(order, projected):
@@ -127,7 +133,8 @@
             pltpu.VMEM((FRAME, TOKG), jnp.bfloat16),
             pltpu.VMEM((1, TOKG), jnp.int32),
             pltpu.VMEM((N_TP, ROWS, FRAME), jnp.bfloat16),
-            pltpu.SemaphoreType.DMA((3,)),
+            pltpu.VMEM((TOKG, TOKG), jnp.bfloat16),
+            pltpu.SemaphoreType.DMA((4,)),
         ],
         cost_estimate=pl.CostEstimate(flops=2 * TOKG * TOKG * FRAME, bytes_accessed=400000, transcendentals=0),
         compiler_params=SMALL,

time: 71.7 us -> 71.7 us (level)
  no operation moved by 1% of the time
where the time goes in v5:
time: 71.7 us; the launch traced here: 71.2 us
  blocking collectives  25.9 us (36%)
  starting transfers between devices  20.7 us (29%)
  waiting for transfers between devices  14.5 us (20%)
  Pallas kernels  8.52 us (12%)
  local copies, waits for them, and re-layouts  0.82 us (1%)
  between operations  0.73 us (1%)
    all_to_all x2, blocking collectives, exchange(): return lax.all_to_all(slots, axis, split_axis=0, concat_axis=0, tiled=True)  25.9 us
    all_to_all x2, starting transfers between devices, exchange(): return lax.all_to_all(slots, axis, split_axis=0, concat_axis=0, tiled=True)  20.7 us
    all_to_all x2, waiting for transfers between devices, exchange(): return lax.all_to_all(slots, axis, split_axis=0, concat_axis=0, tiled=True)  14.5 us
    pallas_call x1, Pallas kernels, attend(): pl.pallas_call(attend_kernel, out_shape=(pltpu.VMEM((KVH, rows, HD), jnp....  3.12 us
    pallas_call x1, Pallas kernels, extract(): pl.pallas_call(extract_kernel, out_shape=(pltpu.VMEM((PIECES, 16, HD), jn...  2.21 us
    pallas_call x1, Pallas kernels, slot_rows(): pl.pallas_call(rows_kernel, out_shape=(jax.ShapeDtypeStruct((N_TP, ROWS,...  1.86 us
  transfers between devices with their start and end apart: 2, of which 2 were waited for; matrix products, arithmetic and copies ran while one was open for 0% of the time, Pallas kernels for 7%

profile of v5, /device:TPU:8, one launch (start us, length us, event | category | flops | bytes accessed | tf_op | source)
XLA Modules:
  0.0 71.2 jit_solution(2860202536028241238)
XLA Ops:
  0.0 1.9 %slot_rows.1 = (bf16[16,16,384]{2,1,0:T(8,128)(2,1)}, bf16[256,256]{1,0:T(8,128)(2,1)S(1)}) custom-call(s32[1,256]{1,0:T(1,128)} %order.1, bf16[1,320,256]{2,1,0:T(8,128)(2,1)} %bitcast.7), custom_call_target="tpu_custom_call" | custom-call | flops 50331648 | bytes 400000 | tf_op jit(solution)/shard_map/slot_rows/pallas_call | solution.py:124
  1.9 8.8 %all-to-all-start.1 = ((bf16[16,16,384]{2,1,0:T(8,128)(2,1)}), bf16[16,16,384]{2,1,0:T(8,128)(2,1)S(1)}, u32[]{:S(2)}, u32[]{:S(2)}) async-start(bf16[16,16,384]{2,1,0:T(8,128)(2,1)} %get-tuple-element.17), calls=%async_computation.1 | async-start | bytes 393216 | tf_op jit(solution)/shard_map/all_to_all | solution.py:298
  11.3 0.0 copy-start.1
  11.3 0.6 copy-done.1
  12.0 0.0 copy-start.3
  12.0 0.0 copy-start.2
  12.0 0.0 copy-start
  12.0 2.2 %extract.1 = (bf16[32,16,128]{2,1,0:T(8,128)(2,1)}, s32[32]{0:T(128)S(4)}) custom-call(s32[1,1]{1,0:T(1,128)S(6)} %copy.11.block_id, s32[32]{0:T(128)S(1)} %copy-done.1, bf16[32,4,16,512]{3,2,1,0:T(8,128)(2,1)} %bitcast.4, bf16[32,4,16,512]{3,2,1,0:T(8,128)(2,1)} %bitcast.5), custom_call_target="tpu_custom_call" | custom-call | tf_op jit(solution)/shard_map/extract/pallas_call | solution.py:58
  14.2 8.6 %all-to-all-done.1.served = bf16[16,16,384]{2,1,0:T(8,128)(2,1)S(1)} async-done(((bf16[16,16,384]{2,1,0:T(8,128)(2,1)}), bf16[16,16,384]{2,1,0:T(8,128)(2,1)S(1)}, u32[]{:S(2)}, u32[]{:S(2)}) %all-to-all-start.1) | async-done | bytes 196640 | tf_op jit(solution)/shard_map/all_to_all | solution.py:298
  22.8 11.9 %all-to-all-start = ((bf16[32,16,128]{2,1,0:T(8,128)(2,1)}), bf16[32,16,128]{2,1,0:T(8,128)(2,1)S(1)}, u32[]{:S(2)}, u32[]{:S(2)}) async-start(bf16[32,16,128]{2,1,0:T(8,128)(2,1)} %get-tuple-element.16), calls=%async_computation | async-start | bytes 262144 | tf_op jit(solution)/shard_map/all_to_all | solution.py:298
  34.7 0.0 copy-done.3
  34.8 0.1 copy.10.lengths
  34.8 0.0 copy-done.2
  34.8 0.1 copy.9.tables
  34.9 0.0 copy-done
  34.9 3.1 %attend.1 = (f32[4,128,128]{2,1,0:T(8,128)S(1)}, f32[4,128,128]{2,1,0:T(8,128)S(1)}, f32[4,128,128]{2,1,0:T(8,128)S(1)}, bf16[4,128,128]{2,1,0:T(8,128)(2,1)S(1)}, f32[16,64]{1,0:T(8,128)S(1)}) custom-call(s32[1,1]{1,0:T(1,128)S(6)} %copy.11.block_id, bf16[16,16,384]{2,1,0:T(8,128)(2,1)S(1)} %all-to-all-done.1.served, bf16[1,32,64,512]{3,2,1,0:T(8,128)(2,1)S(1)} %copy-done, ...), custom_call_target="tpu_custom_call" | custom-call | flops 536870912 | bytes 5000000 | tf_op jit(solution)/shard_map/attend/pallas_call | solution.py:206
  38.0 5.9 %all-to-all-done.got = bf16[32,16,128]{2,1,0:T(8,128)(2,1)S(1)} async-done(((bf16[32,16,128]{2,1,0:T(8,128)(2,1)}), bf16[32,16,128]{2,1,0:T(8,128)(2,1)S(1)}, u32[]{:S(2)}, u32[]{:S(2)}) %all-to-all-start) | async-done | bytes 131104 | tf_op jit(solution)/shard_map/all_to_all | solution.py:298
  44.0 12.5 %all_to_all.20.arrived = bf16[32,16,128]{2,1,0:T(8,128)(2,1)S(1)} all-to-all(bf16[32,16,128]{2,1,0:T(8,128)(2,1)S(1)} %forward.1), channel_id=1, replica_groups=mesh['rep'=32,'tp'=16] {'rep'}, dimensions={0} | all-to-all | bytes 262144 | tf_op jit(solution)/shard_map/all_to_all | solution.py:298
  56.5 0.4 merge.1
  57.0 13.4 %all_to_all.21.returned = bf16[16,16,256]{2,1,0:T(8,128)(2,1)S(1)} all-to-all(bf16[16,16,256]{2,1,0:T(8,128)(2,1)S(1)} %merge.1), channel_id=1, replica_groups=mesh['rep'=32,'tp'=16] {'tp'}, dimensions={0} | all-to-all | bytes 262144 | tf_op jit(solution)/shard_map/all_to_all | solution.py:298
  70.4 0.9 %place.1 = bf16[1,256,256]{2,1,0:T(8,128)(2,1)} custom-call(bf16[256,256]{1,0:T(8,128)(2,1)S(1)} %get-tuple-element.14.chosen, bf16[16,16,256]{2,1,0:T(8,128)(2,1)S(1)} %all_to_all.21.returned), custom_call_target="tpu_custom_call" | custom-call | tf_op jit(solution)/shard_map/place/pallas_call | solution.py:286
  (1 shorter events, 0.0 us)
Async XLA Ops:
  1.9 20.9 %all-to-all-start.1 = ((bf16[16,16,384]{2,1,0:T(8,128)(2,1)}), bf16[16,16,384]{2,1,0:T(8,128)(2,1)S(1)}, u32[]{:S(2)}, u32[]{:S(2)}) async-start(bf16[16,16,384]{2,1,0:T(8,128)(2,1)} %get-tuple-element.17), calls=%async_computation.1 | async-start | bytes 393216 | tf_op jit(solution)/shard_map/all_to_all | solution.py:298
  11.3 0.7 copy-start.1
  12.0 22.8 %copy-start.3 = (s32[1,16]{1,0:T(1,128)S(1)}, s32[1,16]{1,0:T(1,128)}, u32[]{:S(2)}) copy-start(s32[1,16]{1,0:T(1,128)} %param.13) | copy-start | bytes 196
  12.0 22.9 %copy-start.2 = (s32[1,16,8]{1,2,0:T(8,128)S(1)}, s32[1,16,8]{1,2,0:T(8,128)}, u32[]{:S(2)}) copy-start(s32[1,16,8]{1,2,0:T(8,128)} %param.12) | copy-start | bytes 1540
  12.0 23.0 %copy-start = (bf16[1,32,64,512]{3,2,1,0:T(8,128)(2,1)S(1)}, bf16[1,32,64,512]{3,2,1,0:T(8,128)(2,1)}, u32[]{:S(2)}) copy-start(bf16[1,32,64,512]{3,2,1,0:T(8,128)(2,1)} %keys.1) | copy-start | bytes 6291460
  22.8 21.1 %all-to-all-start = ((bf16[32,16,128]{2,1,0:T(8,128)(2,1)}), bf16[32,16,128]{2,1,0:T(8,128)(2,1)S(1)}, u32[]{:S(2)}, u32[]{:S(2)}) async-start(bf16[32,16,128]{2,1,0:T(8,128)(2,1)} %get-tuple-element.16), calls=%async_computation | async-start | bytes 262144 | tf_op jit(solution)/shard_map/all_to_all | solution.py:298
